TPU v7x, 128 devices: a whole 4x4x4 slice. The times are simulated.
128 devices in a mesh: ctx: 8 (over y, core), exp: 16 (over z, x).
Axes of the slice: x: 4, y: 4, z: 4, core: 2. Of those that a mesh axis runs over, the one named last changes fastest.
Arguments:
- tokens: bfloat16 [16, 2048, 1024], P('exp', 'ctx'), may hold values from -6 to 6
- norm_attn: bfloat16 [1024], P(('ctx', 'exp')), may hold values from 0.5 to 1.5
- w_query: bfloat16 [1024, 1024], P(('ctx', 'exp')), may hold values from -0.1875 to 0.1875
- w_key: bfloat16 [1024, 512], P(('ctx', 'exp')), may hold values from -0.1875 to 0.1875
- w_value: bfloat16 [1024, 512], P(('ctx', 'exp')), may hold values from -0.1875 to 0.1875
- w_out: bfloat16 [1024, 1024], P(('ctx', 'exp')), may hold values from -4 to 4
- norm_moe: bfloat16 [1024], P(('ctx', 'exp')), may hold values from 0.5 to 1.5
- w_router: bfloat16 [1024, 32], P(('ctx', 'exp')), may hold values from -0.09375 to 0.09375
- w_gate: bfloat16 [32, 1024, 512], P('exp', 'ctx'), may hold values from -0.1875 to 0.1875
- w_up: bfloat16 [32, 1024, 512], P('exp', 'ctx'), may hold values from -0.1875 to 0.1875
- w_down: bfloat16 [32, 512, 1024], P('exp', None, 'ctx'), may hold values from -1 to 1
- routes: int32 [16, 2048, 8], P('exp', 'ctx'), may hold values from 0 to 31, all different within a row; in each aligned block of 256 rows (0 to 255, 256 to 511, ..., all dimensions but the last counted through in order) at most 96 rows name the same one
- cotangent: bfloat16 [16, 2048, 1024], P('exp', 'ctx'), may hold values from -6 to 6
Outputs:
- output: bfloat16 [16, 2048, 1024], P('exp', 'ctx')
- grad_tokens: bfloat16 [16, 2048, 1024], P('exp', 'ctx')
- grad_norm_attn: float32 [1024], P(('ctx', 'exp'))
- grad_query: float32 [1024, 1024], P(('ctx', 'exp'))
- grad_key: float32 [1024, 512], P(('ctx', 'exp'))
- grad_value: float32 [1024, 512], P(('ctx', 'exp'))
- grad_out_proj: float32 [1024, 1024], P(('ctx', 'exp'))
- grad_norm_moe: float32 [1024], P(('ctx', 'exp'))
- grad_router: float32 [1024, 32], P(('ctx', 'exp'))
- grad_gate: float32 [32, 1024, 512], P('exp', 'ctx')
- grad_up: float32 [32, 1024, 512], P('exp', 'ctx')
- grad_down: float32 [32, 512, 1024], P('exp', None, 'ctx')
Inputs may be any that keep to these rules, and one draw needn't show every extreme that they name: `routes`: each row names 8 different experts. In the rows of one device (each aligned block of 256 rows in order of sequence and position) no expert is named more than 96 times; in some blocks one is named exactly 96 times.
All inputs are finite; a program needn't handle non-finite values.
Results may differ from a plain program's by a relative error of at most 0.038.
Values may be sent and summed in bfloat16 or wider, within the bound.
A program may use at most 192 MiB of HBM per device.

v0:
```python
import jax
import jax.numpy as jnp
from jax import lax
from jax.sharding import PartitionSpec as P

HEADS = 16
HEAD = 64
KV_HEADS = 8
TOP = 8
CAP = 96


EPSILON = 1e-06
PRECISE = lax.Precision.HIGHEST


def sent_together(arrays, axis, dim, along):
    columns = [a.reshape(*a.shape[:along], -1) for a in arrays]
    both = jnp.concatenate(columns, axis=along)
    out, at, outs = (lax.all_gather(both, axis, axis=dim, tiled=True), 0, [])
    for a, column in zip(arrays, columns):
        slab = out[..., at : at + column.shape[along]]
        outs.append(slab.reshape(*slab.shape[:along], *a.shape[along:]))
        at += column.shape[along]
    return tuple(outs)


def sent_together_2(arrays, axis, split_dim, concat_dim, along):
    both = jnp.concatenate(arrays, axis=along)
    out, at, outs = (
        lax.all_to_all(both, axis, split_axis=split_dim, concat_axis=concat_dim, tiled=True),
        0,
        [],
    )
    for a in arrays:
        outs.append(lax.slice_in_dim(out, at, at + a.shape[along], axis=along))
        at += a.shape[along]
    return tuple(outs)


def in_one_piece(arrays, axis, dim, along):
    both = jnp.concatenate(arrays, axis=along)
    out, at, outs = (lax.all_gather(both, axis, axis=dim, tiled=True), 0, [])
    for a in arrays:
        outs.append(lax.slice_in_dim(out, at, at + a.shape[along], axis=along))
        at += a.shape[along]
    return tuple(outs)


def split_up(x, dim, peers):
    before, after = (x.shape[:dim], x.shape[dim + 1 :])
    return jnp.moveaxis(x.reshape(*before, peers, -1, *after), dim, 0)


def in_order(parts, dim):
    parts = jnp.moveaxis(parts, 0, dim)
    dims = parts.shape
    return parts.reshape(*dims[:dim], dims[dim] * dims[dim + 1], *dims[dim + 2 :])


def joined_exchange(x, axis, axes, splits, concats):
    sizes = [lax.axis_size(a) for a in axes]
    parts = split_up(x, splits[0], sizes[0])
    parts = jnp.moveaxis(split_up(parts, splits[1] + 1, sizes[1]), 0, 1)
    inside = parts.shape[2:]
    parts = parts.reshape(-1, *inside)
    parts = lax.all_to_all(parts, axis, split_axis=0, concat_axis=0, tiled=True)
    parts = in_order(parts.reshape(*sizes, *inside), concats[0] + 1)
    return in_order(parts, concats[1])


def sent_together_3(arrays, axis, dim, along):
    widths = [a.shape[along] for a in arrays]
    both = jnp.concatenate(arrays, axis=along)
    out = lax.psum_scatter(both, axis, scatter_dimension=dim, tiled=True)
    return tuple(jnp.split(out, [sum(widths[:k]) for k in range(1, len(widths))], axis=along))


def sum_packed(arrays, axis, dims):
    peers = lax.axis_size(axis)
    parts = [split_up(a, dim, peers) for a, dim in zip(arrays, dims)]
    lines = jnp.concatenate([b.reshape(peers, -1) for b in parts], axis=1)
    rows = max(16, -(-lines.shape[1] // 1024) * 8)
    lines = jnp.pad(lines, ((0, 0), (0, rows * 128 - lines.shape[1]))).reshape(-1, 128)
    flat, at, outs = (lax.psum_scatter(lines, axis, tiled=True).reshape(-1), 0, [])
    for b in parts:
        part = b[0]
        outs.append(flat[at : at + part.size].reshape(part.shape))
        at += part.size
    return tuple(outs)


def rms_scale(values, gain):
    return values * lax.rsqrt(jnp.mean(values * values, axis=-1, keepdims=True) + EPSILON) * gain


def slot_position(flat_routes, experts_total):
    onehot = (flat_routes[:, None] == jnp.arange(experts_total, dtype=jnp.int32)[None, :]).astype(
        jnp.int32
    )
    return jnp.sum((jnp.cumsum(onehot, axis=0) - onehot) * onehot, axis=1)


def spread_layout(route_rows, local_count, owner_count, ctx_count):
    flat_routes = route_rows.reshape(-1)
    position = slot_position(flat_routes, local_count * owner_count)
    replicas = ctx_count // local_count
    piece_slots = CAP // replicas
    owner_index = flat_routes // local_count
    target = flat_routes % local_count * replicas + position % replicas
    return (owner_index * ctx_count + target) * piece_slots + position // replicas


def per_device(
    tokens,
    norm_attn,
    w_query,
    w_key,
    w_value,
    w_out,
    norm_moe,
    w_router,
    w_gate,
    w_up,
    w_down,
    routes,
    cotangent,
):
    token_count = tokens.shape[1]
    model_width = tokens.shape[2]
    ctx_count = lax.axis_size("ctx")
    owner_count = lax.axis_size("exp")
    local_count = w_gate.shape[0]
    group_size = HEADS // KV_HEADS
    score_scale = HEAD ** (-0.5)
    total_slots = local_count * owner_count * CAP
    replicas = ctx_count // local_count
    piece_slots = CAP // replicas
    full_query, full_key, full_value, full_out, full_router, gain_attn, gain_moe = sent_together(
        (w_query, w_key, w_value, w_out, w_router, norm_attn, norm_moe), ("ctx", "exp"), 0, 1
    )
    full_gate, full_up = sent_together_2(
        (jnp.repeat(w_gate, replicas, axis=0), jnp.repeat(w_up, replicas, axis=0)), "ctx", 0, 1, 2
    )
    full_down = lax.all_to_all(
        jnp.repeat(w_down, replicas, axis=0), "ctx", split_axis=0, concat_axis=2, tiled=True
    )
    send_shape = (owner_count, ctx_count, piece_slots, model_width)
    gain_attn = gain_attn.astype(jnp.float32)
    gain_moe = gain_moe.astype(jnp.float32)
    token_rows = tokens[0].astype(jnp.float32)
    attn_in = rms_scale(token_rows, gain_attn).astype(jnp.bfloat16)
    queries = jnp.dot(attn_in, full_query, preferred_element_type=jnp.float32).astype(jnp.bfloat16)
    key_rows = jnp.dot(attn_in, full_key, preferred_element_type=jnp.float32).astype(jnp.bfloat16)
    value_rows = jnp.dot(attn_in, full_value, preferred_element_type=jnp.float32).astype(
        jnp.bfloat16
    )
    query_heads = queries.reshape(token_count, KV_HEADS, group_size, HEAD)
    query_pos = lax.axis_index("ctx") * token_count + jnp.arange(token_count)
    run_max = jnp.full((token_count, KV_HEADS, group_size), -1e30, jnp.float32)
    key_piece, value_piece = in_one_piece((key_rows, value_rows), "ctx", 0, 1)
    key_count = key_piece.shape[0]
    key_heads = key_piece.reshape(key_count, KV_HEADS, HEAD)
    value_heads = value_piece.reshape(key_count, KV_HEADS, HEAD)
    scores = (
        jnp.einsum("qgjd,kgd->qgjk", query_heads, key_heads, preferred_element_type=jnp.float32)
        * score_scale
    )
    causal = (jnp.arange(key_count)[None, :] <= query_pos[:, None])[:, None, None, :]
    scores = jnp.where(causal, scores, -1e30)
    new_max = jnp.maximum(run_max, jnp.max(scores, axis=-1))
    weights = jnp.where(causal, jnp.exp(scores - new_max[..., None]), 0.0)
    new_sum = jnp.sum(weights, axis=-1)
    new_acc = jnp.einsum(
        "qgjk,kgd->qgjd",
        weights.astype(jnp.bfloat16),
        value_heads,
        preferred_element_type=jnp.float32,
    )
    log_sum = new_max + jnp.log(new_sum)
    mixed_exact = new_acc / new_sum[..., None]
    mixed_rows = mixed_exact.reshape(token_count, -1).astype(jnp.bfloat16)
    resid = token_rows + jnp.dot(mixed_rows, full_out, preferred_element_type=jnp.float32)
    moe_in = rms_scale(resid, gain_moe).astype(jnp.bfloat16)
    logits = jnp.dot(moe_in, full_router, preferred_element_type=jnp.float32)
    route_rows = routes[0]
    route_match = (
        route_rows[:, :, None]
        == jnp.arange(local_count * owner_count, dtype=jnp.int32)[None, None, :]
    )
    chosen = jnp.sum(jnp.where(route_match, logits[:, None, :], 0.0), axis=-1)
    gate_weights = jax.nn.softmax(chosen, axis=-1)
    slot_index = spread_layout(route_rows, local_count, owner_count, ctx_count)
    outgoing = (
        jnp.zeros((total_slots, model_width), jnp.bfloat16)
        .at[slot_index]
        .set(jnp.repeat(moe_in, TOP, axis=0))
        .reshape(send_shape)
    )
    arrived = joined_exchange(outgoing, ("ctx", "exp"), ("ctx", "exp"), (1, 0), (1, 0)).reshape(
        1, -1, model_width
    )
    gate_part = jnp.einsum("erd,edf->erf", arrived, full_gate, preferred_element_type=jnp.float32)
    up_part = jnp.einsum("erd,edf->erf", arrived, full_up, preferred_element_type=jnp.float32)
    silu_gate = jax.nn.silu(gate_part)
    hidden = (silu_gate * up_part).astype(jnp.bfloat16)
    produced = jnp.einsum(
        "erf,efd->erd", hidden, full_down, preferred_element_type=jnp.float32
    ).astype(jnp.bfloat16)
    came_back = joined_exchange(
        produced.reshape(send_shape), ("ctx", "exp"), ("ctx", "exp"), (1, 0), (1, 0)
    )
    picked = (
        came_back.reshape(total_slots, model_width)[slot_index]
        .reshape(token_count, TOP, model_width)
        .astype(jnp.float32)
    )
    expert_out = jnp.sum(picked * gate_weights[:, :, None], axis=1)
    output = (resid + expert_out).astype(jnp.bfloat16)[None]
    upstream = cotangent[0].astype(jnp.float32)
    slot_grads = (
        (gate_weights[:, :, None] * upstream[:, None, :])
        .astype(jnp.bfloat16)
        .reshape(-1, model_width)
    )
    outgoing_grads = (
        jnp.zeros((total_slots, model_width), jnp.bfloat16)
        .at[slot_index]
        .set(slot_grads)
        .reshape(send_shape)
    )
    arrived_grads = joined_exchange(
        outgoing_grads, ("ctx", "exp"), ("ctx", "exp"), (1, 0), (1, 0)
    ).reshape(1, -1, model_width)
    hidden_grad = jnp.einsum(
        "erd,efd->erf", arrived_grads, full_down, preferred_element_type=jnp.float32
    )
    down_term = jnp.einsum(
        "erf,erd->efd", hidden, arrived_grads, preferred_element_type=jnp.float32
    )
    gate_sigmoid = jax.nn.sigmoid(gate_part)
    gate_grad = (
        hidden_grad * up_part * gate_sigmoid * (1.0 + gate_part * (1.0 - gate_sigmoid))
    ).astype(jnp.bfloat16)
    up_grad = (hidden_grad * silu_gate).astype(jnp.bfloat16)
    gate_term = jnp.einsum("erd,erf->edf", arrived, gate_grad, preferred_element_type=jnp.float32)
    up_term = jnp.einsum("erd,erf->edf", arrived, up_grad, preferred_element_type=jnp.float32)
    row_grads = (
        jnp.einsum("erf,edf->erd", gate_grad, full_gate, preferred_element_type=jnp.float32)
        + jnp.einsum("erf,edf->erd", up_grad, full_up, preferred_element_type=jnp.float32)
    ).astype(jnp.bfloat16)
    returned_grads = joined_exchange(
        row_grads.reshape(send_shape), ("ctx", "exp"), ("ctx", "exp"), (1, 0), (1, 0)
    )
    gate_parts, up_parts = tuple(
        (
            part.astype(jnp.float32)
            for part in sent_together_2(
                (gate_term.astype(jnp.bfloat16), up_term.astype(jnp.bfloat16)), "ctx", 1, 0, 2
            )
        )
    )
    down_parts = lax.all_to_all(
        down_term.astype(jnp.bfloat16), "ctx", split_axis=2, concat_axis=0, tiled=True
    ).astype(down_term.dtype)
    gate_sum = jnp.sum(
        gate_parts.reshape(local_count, replicas, gate_parts.shape[1], gate_parts.shape[2]), axis=1
    )
    up_sum = jnp.sum(
        up_parts.reshape(local_count, replicas, up_parts.shape[1], up_parts.shape[2]), axis=1
    )
    down_sum = jnp.sum(
        down_parts.reshape(local_count, replicas, down_parts.shape[1], down_parts.shape[2]), axis=1
    )
    slot_back = returned_grads.reshape(total_slots, model_width)[slot_index].reshape(
        token_count, TOP, model_width
    )
    moe_in_grad = jnp.sum(slot_back.astype(jnp.float32), axis=1)
    weight_grad = jnp.sum(upstream[:, None, :] * picked, axis=-1)
    chosen_grad = gate_weights * (
        weight_grad - jnp.sum(gate_weights * weight_grad, axis=-1, keepdims=True)
    )
    logit_grad = jnp.sum(jnp.where(route_match, chosen_grad[:, :, None], 0.0), axis=1)
    router_term = jnp.dot(moe_in.astype(jnp.float32).T, logit_grad, precision=PRECISE)
    moe_in_grad = moe_in_grad + jnp.dot(
        logit_grad, full_router.astype(jnp.float32).T, precision=PRECISE
    )
    unused_moe, pull_moe = jax.vjp(rms_scale, resid, gain_moe)
    resid_grad, norm_moe_term = pull_moe(moe_in_grad)
    resid_grad = resid_grad + upstream
    attn_grad = resid_grad.astype(jnp.bfloat16)
    out_term = jnp.einsum("tq,td->qd", mixed_rows, attn_grad, preferred_element_type=jnp.float32)
    mixed_grad = jnp.einsum(
        "td,qd->tq", attn_grad, full_out, preferred_element_type=jnp.float32
    ).astype(jnp.bfloat16)
    grad_heads = mixed_grad.reshape(token_count, KV_HEADS, group_size, HEAD)
    row_delta = jnp.sum(grad_heads.astype(jnp.float32) * mixed_exact, axis=-1)
    all_keys, all_values = in_one_piece((key_rows, value_rows), "ctx", 0, 1)
    key_blocks = all_keys.reshape(ctx_count, token_count, KV_HEADS, HEAD)
    value_blocks = all_values.reshape(ctx_count, token_count, KV_HEADS, HEAD)
    block_starts = jnp.arange(ctx_count, dtype=jnp.int32) * token_count

    def key_block(query_acc, block):
        key_heads, value_heads, first_row = block
        scores = (
            jnp.einsum("qgjd,kgd->qgjk", query_heads, key_heads, preferred_element_type=jnp.float32)
            * score_scale
        )
        causal = ((first_row + jnp.arange(token_count))[None, :] <= query_pos[:, None])[
            :, None, None, :
        ]
        probs = jnp.where(causal, jnp.exp(scores - log_sum[..., None]), 0.0)
        value_term = jnp.einsum(
            "qgjk,qgjd->kgd",
            probs.astype(jnp.bfloat16),
            grad_heads,
            preferred_element_type=jnp.float32,
        )
        prob_grad = jnp.einsum(
            "qgjd,kgd->qgjk", grad_heads, value_heads, preferred_element_type=jnp.float32
        )
        score_grad = (probs * (prob_grad - row_delta[..., None])).astype(jnp.bfloat16)
        query_acc = (
            query_acc
            + jnp.einsum(
                "qgjk,kgd->qgjd", score_grad, key_heads, preferred_element_type=jnp.float32
            )
            * score_scale
        )
        key_term = (
            jnp.einsum(
                "qgjk,qgjd->kgd", score_grad, query_heads, preferred_element_type=jnp.float32
            )
            * score_scale
        )
        return (query_acc, (key_term, value_term))

    query_acc, (key_terms, value_terms) = lax.scan(
        key_block,
        jnp.zeros((token_count, KV_HEADS, group_size, HEAD), jnp.float32),
        (key_blocks, value_blocks, block_starts),
    )
    key_total, value_total = tuple(
        (
            part.astype(jnp.float32)
            for part in sent_together_3(
                (
                    key_terms.reshape(-1, KV_HEADS * HEAD).astype(jnp.bfloat16),
                    value_terms.reshape(-1, KV_HEADS * HEAD).astype(jnp.bfloat16),
                ),
                "ctx",
                0,
                1,
            )
        )
    )
    query_grad = query_acc.reshape(token_count, -1).astype(jnp.bfloat16)
    key_grad = key_total.astype(jnp.bfloat16)
    value_grad = value_total.astype(jnp.bfloat16)
    attn_in_grad = (
        jnp.einsum("tq,dq->td", query_grad, full_query, preferred_element_type=jnp.float32)
        + jnp.einsum("tk,dk->td", key_grad, full_key, preferred_element_type=jnp.float32)
        + jnp.einsum("tk,dk->td", value_grad, full_value, preferred_element_type=jnp.float32)
    )
    query_term = jnp.einsum("td,tq->dq", attn_in, query_grad, preferred_element_type=jnp.float32)
    key_term_w = jnp.einsum("td,tk->dk", attn_in, key_grad, preferred_element_type=jnp.float32)
    value_term_w = jnp.einsum("td,tk->dk", attn_in, value_grad, preferred_element_type=jnp.float32)
    unused_attn, pull_attn = jax.vjp(rms_scale, token_rows, gain_attn)
    token_grad_part, norm_attn_term = pull_attn(attn_in_grad)
    token_grad = (token_grad_part + resid_grad).astype(jnp.bfloat16)[None]
    query_sum, key_sum, value_sum, out_sum, router_sum, norm_attn_sum, norm_moe_sum = sum_packed(
        (
            query_term,
            key_term_w,
            value_term_w,
            out_term,
            router_term,
            norm_attn_term,
            norm_moe_term,
        ),
        ("ctx", "exp"),
        (0, 0, 0, 0, 0, 0, 0),
    )
    return (
        output,
        token_grad,
        norm_attn_sum,
        query_sum,
        key_sum,
        value_sum,
        out_sum,
        norm_moe_sum,
        router_sum,
        gate_sum,
        up_sum,
        down_sum,
    )


def solution(mesh):
    in_specs = (
        P("exp", "ctx", None),
        P(("ctx", "exp")),
        P(("ctx", "exp"), None),
        P(("ctx", "exp"), None),
        P(("ctx", "exp"), None),
        P(("ctx", "exp"), None),
        P(("ctx", "exp")),
        P(("ctx", "exp"), None),
        P("exp", "ctx", None),
        P("exp", "ctx", None),
        P("exp", None, "ctx"),
        P("exp", "ctx", None),
        P("exp", "ctx", None),
    )
    out_specs = (
        P("exp", "ctx", None),
        P("exp", "ctx", None),
        P(("ctx", "exp")),
        P(("ctx", "exp"), None),
        P(("ctx", "exp"), None),
        P(("ctx", "exp"), None),
        P(("ctx", "exp"), None),
        P(("ctx", "exp")),
        P(("ctx", "exp"), None),
        P("exp", "ctx", None),
        P("exp", "ctx", None),
        P("exp", None, "ctx"),
    )
    return jax.shard_map(
        per_device, mesh=mesh, in_specs=in_specs, out_specs=out_specs, check_vma=False
    )
```

profile of v0, /device:TPU:1, one launch (start us, length us, event | category | flops | bytes accessed | tf_op | source)
XLA Modules:
  0.0 1033.0 jit_solution(8667582482136603292)
XLA Ops:
  11.5 72.1 %all-gather.3.cloned.1.call-done = bf16[1024,3106]{1,0:T(8,128)(2,1)} async-done(((bf16[8,3106]{1,0:T(8,128)(2,1)}), bf16[1024,3106]{1,0:T(8,128)(2,1)}) %all-gather.3.cloned.1.call-update) | async-done | bytes 6361104 | tf_op jit(solution)/shard_map/all_gather | solution.py:20
  96.8 9.1 reduce-window.6
  110.5 25.5 %all-gather.5.cloned.1.call-done = bf16[2048,1024]{1,0:T(8,128)(2,1)} async-done(((bf16[256,1024]{1,0:T(8,128)(2,1)}), bf16[2048,1024]{1,0:T(8,128)(2,1)}) %all-gather.5.cloned.1.call-update) | async-done | bytes 4194320 | tf_op jit(solution)/shard_map/all_gather | solution.py:43
  143.9 15.2 %fusion.33 = (f32[256,8,2]{0,2,1:T(2,128)S(1)}, f32[8,2048,256,2]{2,1,3,0:T(8,128)}) fusion(pred[256,2048]{0,1:T(8,128)(4,1)} %iota_compare_fusion, bf16[2048,8,64,1]{0,2,3,1:T(8,128)(2,1)} %bitcast.358, bf16[256,8,2,64]{0,3,2,1:T(8,128)(2,1)S(1)} %bitcast.347), kind=kOutput, calls=%fused_computation.40 | convolution fusion | flops 1098903552 | bytes 36716544 | tf_op jit(solution)/shard_map/qgjd,kgd->qgjk/dot_general | solution.py:166
  162.2 15.0 %fusion.34 = f32[256,8,2]{0,2,1:T(2,128)S(1)} fusion(f32[8,2048,256,2]{2,1,3,0:T(8,128)} %get-tuple-element.303, f32[256,8,2]{0,2,1:T(2,128)S(1)} %broadcast_maximum_fusion, pred[256,2048]{0,1:T(8,128)(4,1)S(1)} %copy-done.13), kind=kLoop, calls=%fused_computation.41 | loop fusion | flops 41938944 | bytes 34111488 | tf_op jit(solution)/shard_map/reduce_sum | solution.py:173
  177.2 15.7 %fusion.140 = (bf16[256,8,2,64]{0,3,2,1:T(8,128)(2,1)S(1)}, f32[256,8,2,64]{0,3,2,1:T(8,128)}) fusion(f32[256,8,2]{0,2,1:T(2,128)S(1)} %fusion.34, bf16[2048,8,64,1]{0,2,3,1:T(8,128)(2,1)S(1)} %bitcast.380, f32[8,2048,256,2]{2,1,3,0:T(8,128)} %get-tuple-element.303, f32[256,8,2]{0,2,1:T(2,128)S(1)} %broadcast_maximum_fusion, ...), kind=kOutput, calls=%fused_computation.206 | convolution fusion | flops 1116209152 | bytes 37781504 | tf_op jit(solution)/shard_map/qgjk,kgd->qgjd/dot_general | solution.py:174
  196.7 13.5 %scatter_custom_fusion = bf16[3072,1024]{1,0:T(8,128)(2,1)} fusion(s32[2048]{0:T(1024)S(1)} %bitcast.389, bf16[]{:T(256)} %constant.101.clone.1, bf16[256,1024]{1,0:T(8,128)(2,1)S(1)} %multiply_convert_fusion.3), kind=kCustom, calls=%fused_computation.61 | custom fusion | bytes 6815746 | tf_op jit(solution)/shard_map/scatter | solution.py:197
  210.3 6.5 copy.251
  216.7 9.1 all-to-all-start
  228.5 14.5 %scatter_custom_fusion.1 = bf16[3072,1024]{1,0:T(8,128)(2,1)} fusion(s32[2048]{0:T(1024)S(1)} %bitcast.390, f32[256,1024]{1,0:T(8,128)} %bitcast_convert_fusion, f32[2048]{0:T(1024)S(1)} %div.90, bf16[]{:T(256)} %constant.101.clone.1), kind=kCustom, calls=%fused_computation.59 | custom fusion | flops 4194304 | bytes 7348226 | tf_op jit(solution)/shard_map/scatter | solution.py:229
  243.0 6.4 copy.262
  249.4 50.6 %all-to-all-done = bf16[128,1,1,24,1024]{4,3,2,1,0:T(8,128)(2,1)} async-done(((bf16[128,1,1,24,1024]{4,3,2,1,0:T(8,128)(2,1)}), bf16[128,1,1,24,1024]{4,3,2,1,0:T(8,128)(2,1)}, u32[]{:S(2)}, u32[]{:S(2)}) %all-to-all-start) | async-done | bytes 6291488 | tf_op jit(solution)/shard_map/all_to_all | solution.py:67
  300.0 9.4 all-to-all-start.4
  309.6 6.5 copy.253
  316.2 67.8 %all-to-all-done.4 = bf16[128,1,1,24,1024]{4,3,2,1,0:T(8,128)(2,1)} async-done(((bf16[128,1,1,24,1024]{4,3,2,1,0:T(8,128)(2,1)}), bf16[128,1,1,24,1024]{4,3,2,1,0:T(8,128)(2,1)}, u32[]{:S(2)}, u32[]{:S(2)}) %all-to-all-start.4) | async-done | bytes 6291488 | tf_op jit(solution)/shard_map/all_to_all | solution.py:67
  390.1 9.1 fusion.91
  399.2 6.4 copy.264
  405.6 9.1 fusion.92
  414.7 12.7 %multiply_convert_fusion = (bf16[3072,512]{1,0:T(8,128)(2,1)}, bf16[3072,512]{1,0:T(8,128)(2,1)}, bf16[3072,512]{1,0:T(8,128)(2,1)S(1)}) fusion(f32[3072,512]{1,0:T(8,128)} %fusion.91, f32[3072,512]{1,0:T(8,128)} %fusion.92, bf16[3072,1024]{1,0:T(8,128)(2,1)} %bitcast.370, bf16[512,1024]{0,1:T(8,128)(2,1)} %bitcast.34), kind=kOutput, calls=%fused_computation.53 | convolution fusion | flops 3244818432 | bytes 29360128 | tf_op jit(solution)/shard_map/erd,efd->erf/dot_general | solution.py:235
  427.4 5.7 convolution_convert_fusion
  436.4 9.9 all-to-all-start.3
  446.3 10.4 %fusion.90 = f32[3072,1024]{1,0:T(8,128)} fusion(bf16[3072,512]{1,0:T(8,128)(2,1)} %get-tuple-element.294, bf16[1,1024,1024]{2,1,0:T(8,128)(2,1)} %bitcast.28), kind=kOutput, calls=%fused_computation.124 | convolution fusion | flops 3221225472 | bytes 16777216 | tf_op jit(solution)/shard_map/erf,edf->erd/dot_general | solution.py:249
  456.7 6.8 add_convert_fusion
  466.9 53.9 %all-to-all-done.3 = bf16[128,1,1,24,1024]{4,3,2,1,0:T(8,128)(2,1)} async-done(((bf16[128,1,1,24,1024]{4,3,2,1,0:T(8,128)(2,1)}), bf16[128,1,1,24,1024]{4,3,2,1,0:T(8,128)(2,1)}, u32[]{:S(2)}, u32[]{:S(2)}) %all-to-all-start.3) | async-done | bytes 6291488 | tf_op jit(solution)/shard_map/all_to_all | solution.py:67
  520.8 9.3 all-to-all-start.5
  530.4 6.2 reshape.756
  549.4 6.4 copy.257
  555.8 14.6 %gather_fusion = bf16[2048,1024]{1,0:T(8,128)(2,1)} fusion(bf16[3072,1024]{1,0:T(8,128)(2,1)} %bitcast.346, s32[2048]{0:T(1024)S(1)} %broadcast_clamp_fusion), kind=kCustom, calls=%fused_computation | custom fusion | bytes 8396800 | tf_op jit(solution)/shard_map/gather | solution.py:214
  570.4 6.2 fusion.40
  576.7 27.9 %all-to-all-done.5 = bf16[128,1,1,24,1024]{4,3,2,1,0:T(8,128)(2,1)} async-done(((bf16[128,1,1,24,1024]{4,3,2,1,0:T(8,128)(2,1)}), bf16[128,1,1,24,1024]{4,3,2,1,0:T(8,128)(2,1)}, u32[]{:S(2)}, u32[]{:S(2)}) %all-to-all-start.5) | async-done | bytes 6291488 | tf_op jit(solution)/shard_map/all_to_all | solution.py:67
  604.6 6.5 copy.267
  611.1 14.8 %gather_fusion.1 = bf16[2048,1024]{1,0:T(8,128)(2,1)} fusion(bf16[3072,1024]{1,0:T(8,128)(2,1)} %bitcast.345, s32[2048]{0:T(1024)S(1)} %broadcast_clamp_fusion), kind=kCustom, calls=%fused_computation.1 | custom fusion | bytes 8396800 | tf_op jit(solution)/shard_map/gather | solution.py:275
  641.4 99.7 %while.15 = (s32[]{:T(128)}, f32[256,8,2,64]{0,3,2,1:T(8,128)}, bf16[8,256,8,64]{1,3,2,0:T(8,128)(2,1)}, bf16[8,256,8,64]{1,3,2,0:T(8,128)(2,1)}, bf16[8,256,8,6...) while((s32[]{:T(128)}, f32[256,8,2,64]{0,3,2,1:T(8,128)}, ...), condition=%wide.region_20.21_spmd.clone, body=%wide.region_19.20_spmd.clone.sunk | while | flops 682557952 | bytes 75487504 | solution.py:338
  773.0 12.0 %reduce-scatter.2.cloned.1.call-done = bf16[256,1024]{0,1:T(8,128)(2,1)} async-done(((bf16[2048,1024]{0,1:T(8,128)(2,1)}), bf16[256,1024]{0,1:T(8,128)(2,1)}) %reduce-scatter.2.cloned.1.call-update) | async-done | bytes 524304 | tf_op jit(solution)/shard_map/reduce_scatter | solution.py:75
  800.4 15.3 %concatenate.23 = f32[128,24848]{1,0:T(8,128)} concatenate(f32[128,8192]{1,0:T(8,128)} %reshape_reshape.47, f32[128,4096]{1,0:T(8,128)} %reshape_reshape.48, f32[128,4096]{1,0:T(8,128)} %reshape_reshape.49, f32[128,8192]{1,0:T(8,128)} %reshape_reshape.50, f32[128,256]{1,0:T(8,128)S(1)} %reshape_reshape.51, f32[128,8]{1,0:T(8,128)S(1)} %reshape.693, f32[128,8]{1,0:T(8,128)S(1)} %reshape.694), dimensions={1} | concatenate | bytes 25444352 | tf_op jit(solution)/shard_map/concatenate | solution.py:82
  815.6 10.7 %pad.4 = f32[128,25600]{1,0:T(8,128)} pad(f32[128,24848]{1,0:T(8,128)} %concatenate.23, f32[]{:T(128)} %constant.92.clone.1), padding=0_0x0_752 | pad | bytes 25829380 | tf_op jit(solution)/shard_map/jit(_pad)/pad | solution.py:84
  826.4 12.1 %reshape.695 = f32[25600,128]{1,0:T(8,128)} reshape(f32[128,25600]{1,0:T(8,128)} %pad.4) | data formatting | bytes 26214400 | tf_op jit(solution)/shard_map/reshape | solution.py:84
  838.5 7.2 fusion.62
  850.3 8.0 reduce.9
  859.9 7.4 all-to-all-start.7
  867.3 7.6 fusion.60
  874.9 6.4 fusion.61
  882.8 10.9 %copy.276 = bf16[1,1024,1024]{2,0,1:T(2,128)(2,1)} copy(bf16[1,1024,1024]{1,2,0:T(8,128)(2,1)} %pad_maximum_fusion.2) | data formatting | bytes 4194304 | tf_op jit(solution)/shard_map/concatenate | solution.py:29
  893.8 14.1 %reduce.8 = bf16[1024,1024]{1,0:T(8,128)(2,1)} reduce(bf16[1024,1,1024]{2,1,0:T(2,128)(2,1)} %bitcast.355, bf16[]{:T(256)} %broadcast.463), dimensions={1}, to_apply=%bitcast.273.reduce_sub_computation | reduce | bytes 4194306
  907.8 6.3 reshape.764
  936.0 11.6 %all-to-all-done.6 = bf16[8,2,65536]{2,1,0:T(2,128)(2,1)} async-done(((bf16[8,2,65536]{2,1,0:T(2,128)(2,1)}), bf16[8,2,65536]{2,1,0:T(2,128)(2,1)}, u32[]{:S(2)}, u32[]{:S(2)}) %all-to-all-start.6) | async-done | bytes 2097184 | tf_op jit(solution)/shard_map/all_to_all | solution.py:31
  947.6 6.8 reshape.765
  959.9 59.4 %all-reduce.4.cloned.1.call-done = f32[25600,128]{1,0:T(8,128)} async-done(((f32[25600,128]{1,0:T(8,128)}), f32[25600,128]{1,0:T(8,128)}) %all-reduce.4.cloned.1.call-update) | async-done | bytes 13107216
  (322 shorter events, 269.3 us)
Async XLA Ops:
  7.2 76.5 %all-gather.3.cloned.1.call-start = ((), (), s32[]{:S(2)}) async-start(), calls=%async_computation.9 | async-start | bytes 6604800 | tf_op jit(solution)/shard_map/all_gather | solution.py:20
  8.7 81.1 %copy-start.24 = (bf16[2,128,512]{2,1,0:T(8,128)(2,1)S(1)}, bf16[2,128,512]{2,1,0:T(8,128)(2,1)}, u32[]{:S(2)}) copy-start(bf16[2,128,512]{2,1,0:T(8,128)(2,1)} %param.23) | copy-start | bytes 786436
  10.2 125.8 %all-gather.5.cloned.1.call-start = ((), (), s32[]{:S(2)}) async-start(), calls=%async_computation.10 | async-start | bytes 4718592 | tf_op jit(solution)/shard_map/all_gather | solution.py:43
  11.5 73.6 %copy-start.34 = (f32[256]{0:T(256)}, f32[256]{0:T(256)S(1)}, u32[]{:S(2)}) copy-start(f32[256]{0:T(256)S(1)} %fusion.83) | copy-start | bytes 3076
  11.5 96.4 %copy-start.32 = (f32[256]{0:T(256)}, f32[256]{0:T(256)S(1)}, u32[]{:S(2)}) copy-start(f32[256]{0:T(256)S(1)} %fusion.128) | copy-start | bytes 3076
  85.1 22.9 %copy-start.29 = (f32[1024]{0:T(1024)}, f32[1024]{0:T(1024)S(1)}, u32[]{:S(2)}) copy-start(f32[1024]{0:T(1024)S(1)} %get-tuple-element.254) | copy-start | bytes 12292
  85.1 4.8 copy-start.25
  90.0 6.2 copy-start.31
  91.7 16.3 %copy-start.5 = (bf16[1,256,1024]{2,1,0:T(8,128)(2,1)S(1)}, bf16[1,256,1024]{2,1,0:T(8,128)(2,1)}, u32[]{:S(2)}) copy-start(bf16[1,256,1024]{2,1,0:T(8,128)(2,1)} %param.15) | copy-start | bytes 1572868
  91.7 125.1 %all-to-all-start.1 = ((bf16[8,128,1024]{2,1,0:T(8,128)(2,1)}), bf16[8,128,1024]{2,1,0:T(8,128)(2,1)}, u32[]{:S(2)}, u32[]{:S(2)}) async-start(bf16[8,128,1024]{2,1,0:T(8,128)(2,1)} %pad_maximum_fusion.1), calls=%async_computation.1 | async-start | bytes 4194304 | tf_op jit(solution)/shard_map/all_to_all | solution.py:31
  110.5 33.3 %copy-start.2 = (bf16[256,1024]{0,1:T(8,128)(2,1)}, bf16[256,1024]{0,1:T(8,128)(2,1)S(1)}, u32[]{:S(2)}) copy-start(bf16[256,1024]{0,1:T(8,128)(2,1)S(1)} %copy.244) | copy-start | bytes 1572868
  159.1 3.1 copy-start.13
  162.2 15.0 %copy-start.18 = (bf16[2048,512]{0,1:T(8,128)(2,1)S(1)}, bf16[2048,512]{0,1:T(8,128)(2,1)}, u32[]{:S(2)}) copy-start(bf16[2048,512]{0,1:T(8,128)(2,1)} %copy.242) | copy-start | bytes 6291460
  192.8 3.9 copy-start.20
  196.7 30.2 %copy-start.14 = (bf16[256,1024]{1,0:T(8,128)(2,1)}, bf16[256,1024]{1,0:T(8,128)(2,1)S(1)}, u32[]{:S(2)}) copy-start(bf16[256,1024]{1,0:T(8,128)(2,1)S(1)} %multiply_convert_fusion.3) | copy-start | bytes 1572868
  216.7 9.1 copy-start.19
  216.7 83.3 %all-to-all-start = ((bf16[128,1,1,24,1024]{4,3,2,1,0:T(8,128)(2,1)}), bf16[128,1,1,24,1024]{4,3,2,1,0:T(8,128)(2,1)}, u32[]{:S(2)}, u32[]{:S(2)}) async-start(bf16[128,1,1,24,1024]{4,3,2,1,0:T(8,128)(2,1)} %bitcast.350), calls=%async_computation | async-start | bytes 12582912 | tf_op jit(solution)/shard_map/all_to_all | solution.py:67
  300.0 9.4 copy-start.26
  300.0 83.9 %all-to-all-start.4 = ((bf16[128,1,1,24,1024]{4,3,2,1,0:T(8,128)(2,1)}), bf16[128,1,1,24,1024]{4,3,2,1,0:T(8,128)(2,1)}, u32[]{:S(2)}, u32[]{:S(2)}) async-start(bf16[128,1,1,24,1024]{4,3,2,1,0:T(8,128)(2,1)} %bitcast.351), calls=%async_computation.4 | async-start | bytes 12582912 | tf_op jit(solution)/shard_map/all_to_all | solution.py:67
  385.0 29.7 %all-to-all-start.2 = ((bf16[8,512,128]{1,2,0:T(8,128)(2,1)}), bf16[8,512,128]{1,2,0:T(8,128)(2,1)}, u32[]{:S(2)}, u32[]{:S(2)}) async-start(bf16[8,512,128]{1,2,0:T(8,128)(2,1)} %bitcast.374), calls=%async_computation.2 | async-start | bytes 2097152 | tf_op jit(solution)/shard_map/all_to_all | solution.py:145
  427.3 5.7 copy-start.38
  436.4 84.4 %all-to-all-start.3 = ((bf16[128,1,1,24,1024]{4,3,2,1,0:T(8,128)(2,1)}), bf16[128,1,1,24,1024]{4,3,2,1,0:T(8,128)(2,1)}, u32[]{:S(2)}, u32[]{:S(2)}) async-start(bf16[128,1,1,24,1024]{4,3,2,1,0:T(8,128)(2,1)} %bitcast.352), calls=%async_computation.3 | async-start | bytes 12582912 | tf_op jit(solution)/shard_map/all_to_all | solution.py:67
  446.3 10.4 %copy-start.36 = (bf16[3072,512]{1,0:T(8,128)(2,1)S(1)}, bf16[3072,512]{1,0:T(8,128)(2,1)}, u32[]{:S(2)}) copy-start(bf16[3072,512]{1,0:T(8,128)(2,1)} %get-tuple-element.293) | copy-start | bytes 9437188
  520.8 83.8 %all-to-all-start.5 = ((bf16[128,1,1,24,1024]{4,3,2,1,0:T(8,128)(2,1)}), bf16[128,1,1,24,1024]{4,3,2,1,0:T(8,128)(2,1)}, u32[]{:S(2)}, u32[]{:S(2)}) async-start(bf16[128,1,1,24,1024]{4,3,2,1,0:T(8,128)(2,1)} %bitcast.349), calls=%async_computation.5 | async-start | bytes 12582912 | tf_op jit(solution)/shard_map/all_to_all | solution.py:67
  530.1 254.9 %reduce-scatter.2.cloned.1.call-start = ((), (), s32[]{:S(2)}) async-start(), calls=%async_computation.11 | async-start | bytes 4718592 | tf_op jit(solution)/shard_map/reduce_scatter | solution.py:75
  544.2 5.1 copy-start.28
  625.8 5.6 copy-start.8
  625.8 7.6 copy-start.16
  634.6 6.8 copy-start.3
  661.6 2.9 copy-start.1
  674.1 2.9 copy-start.1
  699.0 2.9 copy-start.1
  711.5 2.9 copy-start.1
  724.0 2.9 copy-start.1
  736.5 2.9 copy-start.1
  741.1 3.7 copy-start.17
  749.3 270.0 %all-reduce.4.cloned.1.call-start = ((), (), s32[]{:S(2)}) async-start(), calls=%async_computation.12 | async-start | bytes 26214400
  753.3 5.6 copy-start.15
  753.3 8.3 copy-start.4
  753.3 8.4 copy-start.6
  753.3 8.4 copy-start.30
  753.3 8.4 copy-start.33
  785.0 5.7 copy-start.22
  859.9 54.3 %all-to-all-start.7 = ((bf16[8,2,32768]{2,1,0:T(2,128)(2,1)}), bf16[8,2,32768]{2,1,0:T(2,128)(2,1)S(1)}, u32[]{:S(2)}, u32[]{:S(2)}) async-start(bf16[8,2,32768]{2,1,0:T(2,128)(2,1)} %reshape.766), calls=%async_computation.8 | async-start | bytes 2097152 | tf_op jit(solution)/shard_map/all_to_all | solution.py:263
  867.3 7.6 copy-start.37
  914.1 33.5 %all-to-all-start.6 = ((bf16[8,2,65536]{2,1,0:T(2,128)(2,1)}), bf16[8,2,65536]{2,1,0:T(2,128)(2,1)}, u32[]{:S(2)}, u32[]{:S(2)}) async-start(bf16[8,2,65536]{2,1,0:T(2,128)(2,1)} %reshape.764), calls=%async_computation.7 | async-start | bytes 4194304 | tf_op jit(solution)/shard_map/all_to_all | solution.py:31
  954.4 4.3 copy-start.35
  954.4 4.3 copy-start.23
  (31 other events, 57.0 us)
Sparse Core Ops, SparseCore 0:
  11.4 72.1 all-gather.2
  90.0 46.0 all-gather.4
  749.4 35.4 reduce-scatter.1
  838.6 180.6 all-reduce.3
where the time goes:
time: 1050 us; the launch traced here: 1030 us
  waiting for transfers between devices  381 us (36%)
  local copies, waits for them, and re-layouts  259 us (25%)
  matrix products  213 us (20%)
  other arithmetic  104 us (10%)
  starting transfers between devices  60.4 us (6%)
  between operations  14.8 us (1%)
    all_to_all x4, waiting for transfers between devices, joined_exchange(): parts = lax.all_to_all(parts, axis, split_axis=0, concat_axis=0, tiled=True)  200 us
    all_gather x1, waiting for transfers between devices, sent_together(): out, at, outs = (lax.all_gather(both, axis, axis=dim, tiled=True), 0, [])  72.1 us
    unnamed x5, waiting for transfers between devices  59.5 us
    all_to_all x4, starting transfers between devices, joined_exchange(): parts = lax.all_to_all(parts, axis, split_axis=0, concat_axis=0, tiled=True)  37.7 us
    unnamed x83, local copies, waits for them, and re-layouts  37.4 us
    transpose x4, local copies, waits for them, and re-layouts, in_order(): parts = jnp.moveaxis(parts, 0, dim)  25.8 us
    all_gather x1, waiting for transfers between devices, in_one_piece(): out, at, outs = (lax.all_gather(both, axis, axis=dim, tiled=True), 0, [])  25.5 us
    dot_general x8, matrix products, key_block(): jnp.einsum('qgjk,kgd->qgjd', score_grad, key_heads, preferred_element_typ...  22.8 us
  transfers between devices with their start and end apart: 12, of which 9 were waited for; matrix products, arithmetic and copies ran while one was open for 33% of the time, Pallas kernels for 0%

commit v1 on v0

v1 whole, which is shorter than its diff:
```python
import jax
import jax.numpy as jnp
from jax import lax
from jax.experimental import pallas as pl
from jax.experimental.pallas import tpu as pltpu
from jax.sharding import PartitionSpec as P

EPSILON = 1e-06
PRECISE = lax.Precision.HIGHEST
F32, BF16 = jnp.float32, jnp.bfloat16
VMEM = pltpu.VMEM
MESH = pl.DeviceIdType.MESH
SIDE = 4
ROWS = 256
CAP = 96
GROUP = 4


def exp_block(first, second, half, inner):
    index = lax.axis_index("exp")
    z, x = lax.div(index, SIDE), lax.rem(index, SIDE)
    by_x, by_z = (first, second) if half == inner else (second, first)
    return lax.rem(z + by_z + SIDE, SIDE) * SIDE + lax.rem(x + by_x + SIDE, SIDE)


def greet_exp():
    barrier = pltpu.get_barrier_semaphore()
    for half in range(2):
        for step in (1, -1):
            pl.semaphore_signal(
                barrier, inc=1, device_id={"exp": exp_block(step, 0, half, 0)}, device_id_type=MESH
            )
    pl.semaphore_wait(barrier, 4)


def gather_exp_copy(own, out, send, recv, rows, half, axis, k, s):
    part = rows // 4
    step = (1, -1, 1, -1)[s]
    off = (0, 0, -1, 1)[s]
    origin = exp_block(off, 0, half, 0) if axis == 1 else exp_block(k, off, half, 0)
    target = exp_block(step, 0, half, 0) if axis == 1 else exp_block(0, step, half, 0)
    lines = (
        pl.ds(half * 2 * part, 2 * part)
        if s < 2
        else pl.ds((half * 2 + s - 2) * part, part)
    )
    mine = s < 2 and (axis == 1 or k == 0)
    at = half * 20 + (s if axis == 1 else 4 + 4 * (k % 4) + s)
    return pltpu.make_async_remote_copy(
        src_ref=own.at[lines] if mine else out.at[origin, lines],
        dst_ref=out.at[origin, lines],
        send_sem=send.at[at],
        recv_sem=recv.at[at],
        device_id={"exp": target},
        device_id_type=MESH,
    )


def gather_exp_kernel(own, out, send, recv, local):
    rows = own.shape[0]
    greet_exp()
    copies = {
        (half, axis, k, s): gather_exp_copy(own, out, send, recv, rows, half, axis, k, s)
        for half in range(2)
        for axis, k in ((1, 0), (2, 0), (2, 1), (2, -1), (2, 2))
        for s in range(4)
    }
    keep = pltpu.make_async_copy(own, out.at[exp_block(0, 0, 0, 0)], local)
    keep.start()
    for axis in (1, 2):
        for s in (0, 1):
            for half in range(2):
                copies[half, axis, 0, s].start()
    for s, k in ((0, -1), (1, 1)):
        for half in range(2):
            copies[half, 1, 0, s].wait_recv()
            copies[half, 1, 0, s + 2].start()
            copies[half, 2, k, 0].start()
            copies[half, 2, k, 1].start()
    for s in (0, 1):
        for half in range(2):
            copies[half, 2, 0, s].wait_recv()
            copies[half, 2, 0, s + 2].start()
    for half in range(2):
        copies[half, 1, 0, 2].wait_recv()
        copies[half, 1, 0, 3].wait_recv()
        copies[half, 2, 2, 0].start()
        copies[half, 2, 2, 1].start()
    for k in (-1, 1, 2):
        for s in (0, 1):
            for half in range(2):
                copies[half, 2, k, s].wait_recv()
                copies[half, 2, k, s + 2].start()
    for k in (0, -1, 1, 2):
        for s in (2, 3):
            for half in range(2):
                copies[half, 2, k, s].wait_recv()
    for copy in copies.values():
        copy.wait_send()
    keep.wait()


def gather_exp(block, collective_id):
    rows, width = block.shape
    return pl.pallas_call(
        gather_exp_kernel,
        out_shape=jax.ShapeDtypeStruct((16, rows, width), block.dtype),
        in_specs=[pl.BlockSpec(memory_space=pl.ANY)],
        out_specs=pl.BlockSpec(memory_space=pl.ANY),
        scratch_shapes=[
            pltpu.SemaphoreType.DMA((40,)),
            pltpu.SemaphoreType.DMA((40,)),
            pltpu.SemaphoreType.DMA,
        ],
        compiler_params=pltpu.CompilerParams(collective_id=collective_id, has_side_effects=True),
    )(block)


def reduce_exp_copy(parts, landed, send, recv, half, axis, k, s):
    step = (1, -1, 1, -1)[s]
    dest = (2, 2, 1, -1)[s]
    block = exp_block(dest, k, half, 1) if axis == 1 else exp_block(0, dest, half, 1)
    target = exp_block(step, 0, half, 1) if axis == 1 else exp_block(0, step, half, 1)
    row = half * 5 + (k % 4 if axis == 1 else 4)
    source = (
        parts.at[block, pl.ds(2 * half + s, 1)] if s < 2 else parts.at[block, pl.ds(2 * half, 2)]
    )
    place = (pl.ds(0, 1), pl.ds(1, 1), pl.ds(2, 2), pl.ds(4, 2))[s]
    at = row * 4 + s
    return pltpu.make_async_remote_copy(
        src_ref=source,
        dst_ref=landed.at[row, place],
        send_sem=send.at[at],
        recv_sem=recv.at[at],
        device_id={"exp": target},
        device_id_type=MESH,
    )


def add_lines(total, others, step):
    lines = total.shape[0]

    @pl.loop(0, lines // step)
    def _(i):
        at = pl.ds(pl.multiple_of(i * step, step), step)
        value = total[at].astype(jnp.float32)
        for other in others:
            value = value + other[at].astype(jnp.float32)
        total[at] = value.astype(total.dtype)


def reduce_exp_kernel(given, out, parts, landed, send, recv, local, done):
    greet_exp()
    lines = given.shape[2]
    step = 16
    load = pltpu.make_async_copy(given, parts, local)
    load.start()
    load.wait()
    copies = {
        (half, axis, k, s): reduce_exp_copy(parts, landed, send, recv, half, axis, k, s)
        for half in range(2)
        for axis, k in ((1, 0), (1, 1), (1, -1), (1, 2), (2, 0))
        for s in range(4)
    }

    def row_of(half, axis, k):
        return half * 5 + (k % 4 if axis == 1 else 4)

    def block_of(half, axis, k, dest):
        return exp_block(dest, k, half, 1) if axis == 1 else exp_block(0, dest, half, 1)

    def pass_on(half, axis, k):
        for s, dest in ((0, 1), (1, -1)):
            copies[half, axis, k, s].wait_recv()
            add_lines(
                parts.at[block_of(half, axis, k, dest), 2 * half + s],
                [landed.at[row_of(half, axis, k), s]],
                step,
            )
            copies[half, axis, k, s + 2].start()

    def finish(half, axis, k):
        copies[half, axis, k, 2].wait_recv()
        copies[half, axis, k, 3].wait_recv()
        for part in range(2):
            add_lines(
                parts.at[block_of(half, axis, k, 0), 2 * half + part],
                [
                    landed.at[row_of(half, axis, k), 2 + part],
                    landed.at[row_of(half, axis, k), 4 + part],
                ],
                step,
            )

    order = (2, 1, -1, 0)
    for k in order:
        for half in range(2):
            for s in (0, 1):
                copies[half, 1, k, s].start()
    for k in order:
        for half in range(2):
            pass_on(half, 1, k)
    for k in order:
        for half in range(2):
            finish(half, 1, k)
            if k == 2:
                copies[half, 2, 0, 0].start()
                copies[half, 2, 0, 1].start()
    for half in range(2):
        pass_on(half, 2, 0)
    for half in range(2):
        finish(half, 2, 0)
    store = pltpu.make_async_copy(parts.at[exp_block(0, 0, 0, 0)], out, done)
    store.start()
    for copy in copies.values():
        copy.wait_send()
    store.wait()


def reduce_exp(parts, collective_id):
    _, quarters, lines, width = parts.shape
    return pl.pallas_call(
        reduce_exp_kernel,
        out_shape=jax.ShapeDtypeStruct((quarters, lines, width), parts.dtype),
        in_specs=[pl.BlockSpec(memory_space=pl.ANY)],
        out_specs=pl.BlockSpec(memory_space=pl.ANY),
        scratch_shapes=[
            pltpu.VMEM(parts.shape, parts.dtype),
            pltpu.VMEM((10, 6, lines, width), parts.dtype),
            pltpu.SemaphoreType.DMA((40,)),
            pltpu.SemaphoreType.DMA((40,)),
            pltpu.SemaphoreType.DMA,
            pltpu.SemaphoreType.DMA,
        ],
        compiler_params=pltpu.CompilerParams(
            collective_id=collective_id, has_side_effects=True, vmem_limit_bytes=40 << 20
        ),
    )(parts)


def ctx_block(step, other):
    index = lax.axis_index("ctx")
    y, core = lax.div(index, 2), lax.rem(index, 2)
    if other:
        core = 1 - core
    return lax.rem(y + step + SIDE, SIDE) * 2 + core


def greet_ctx():
    barrier = pltpu.get_barrier_semaphore()
    for step, other in ((1, False), (-1, False), (0, True)):
        pl.semaphore_signal(
            barrier, inc=1, device_id={"ctx": ctx_block(step, other)}, device_id_type=MESH
        )
    pl.semaphore_wait(barrier, 3)


def gather_ctx_copies(own, out, send, recv):
    half = own.shape[0] // 2
    every, first, second = pl.ds(0, 2 * half), pl.ds(0, half), pl.ds(half, half)
    plan = (
        (0, every, 0, True),
        (0, every, 1, False),
        (0, every, -1, False),
        (-1, first, 1, False),
        (1, second, -1, False),
        (-1, every, 0, True),
        (1, every, 0, True),
        (2, first, 0, True),
        (2, second, 0, True),
    )
    copies = []
    for at, (origin, lines, step, other) in enumerate(plan):
        slot = out.at[ctx_block(origin, False), lines]
        copies.append(
            pltpu.make_async_remote_copy(
                src_ref=own.at[lines] if origin == 0 else slot,
                dst_ref=slot,
                send_sem=send.at[at],
                recv_sem=recv.at[at],
                device_id={"ctx": ctx_block(step, other)},
                device_id_type=MESH,
            )
        )
    return copies


def gather_ctx_kernel(own, out, send, recv, local):
    greet_ctx()
    copies = gather_ctx_copies(own, out, send, recv)
    for at in (1, 2, 0):
        copies[at].start()
    keep = pltpu.make_async_copy(own, out.at[ctx_block(0, False)], local)
    keep.start()
    for arrival, follow in ((1, (3, 5)), (2, (4, 6)), (3, (7,)), (4, (8,))):
        copies[arrival].wait_recv()
        for at in follow:
            copies[at].start()
    for at in (0, 5, 6, 7, 8):
        copies[at].wait_recv()
    for copy in copies:
        copy.wait_send()
    keep.wait()


def gather_ctx(block, collective_id):
    return pl.pallas_call(
        gather_ctx_kernel,
        out_shape=jax.ShapeDtypeStruct((8,) + block.shape, block.dtype),
        in_specs=[pl.BlockSpec(memory_space=pl.ANY)],
        out_specs=pl.BlockSpec(memory_space=pl.ANY),
        scratch_shapes=[
            pltpu.SemaphoreType.DMA((9,)),
            pltpu.SemaphoreType.DMA((9,)),
            pltpu.SemaphoreType.DMA,
        ],
        compiler_params=pltpu.CompilerParams(collective_id=collective_id, has_side_effects=True),
    )(block)


def reduce_ctx_kernel(given, out, parts, landed, near, send, recv, local, done):
    lines = given.shape[1]
    half = lines // 2
    greet_ctx()
    first, second, every = pl.ds(0, half), pl.ds(half, half), pl.ds(0, lines)

    def remote(src, dst, at, step, other):
        return pltpu.make_async_remote_copy(
            src_ref=src,
            dst_ref=dst,
            send_sem=send.at[at],
            recv_sem=recv.at[at],
            device_id={"ctx": ctx_block(step, other)},
            device_id_type=MESH,
        )

    swaps, loads = {}, {}
    for at, step in enumerate((2, 1, -1, 0)):
        swaps[step] = remote(given.at[ctx_block(step, True)], near.at[at], at, 0, True)
        swaps[step].start()
        loads[step] = pltpu.make_async_copy(
            given.at[ctx_block(step, False)], parts.at[at], local.at[at]
        )
        loads[step].start()
    hops = (
        remote(parts.at[0, first], landed.at[0, first], 4, 1, False),
        remote(parts.at[0, second], landed.at[0, second], 5, -1, False),
        remote(parts.at[1], landed.at[1], 6, 1, False),
        remote(parts.at[2], landed.at[2], 7, -1, False),
    )
    for at, step in enumerate((2, 1, -1, 0)):
        loads[step].wait()
        swaps[step].wait_recv()
        add_lines(parts.at[at], [near.at[at]], 16)
        if step == 2:
            hops[0].start()
            hops[1].start()
        if step == 1:
            hops[0].wait_recv()
            add_lines(parts.at[1, first], [landed.at[0, first]], 16)
            hops[2].start()
        if step == -1:
            hops[1].wait_recv()
            add_lines(parts.at[2, second], [landed.at[0, second]], 16)
            hops[3].start()
    hops[2].wait_recv()
    hops[3].wait_recv()
    add_lines(parts.at[3], [landed.at[1], landed.at[2]], 16)
    store = pltpu.make_async_copy(parts.at[3], out, done)
    store.start()
    for copy in (*swaps.values(), *hops):
        copy.wait_send()
    store.wait()


def reduce_ctx(parts, collective_id):
    _, lines, width = parts.shape
    return pl.pallas_call(
        reduce_ctx_kernel,
        out_shape=jax.ShapeDtypeStruct((lines, width), parts.dtype),
        in_specs=[pl.BlockSpec(memory_space=pl.ANY)],
        out_specs=pl.BlockSpec(memory_space=pl.ANY),
        scratch_shapes=[
            pltpu.VMEM((4, lines, width), parts.dtype),
            pltpu.VMEM((3, lines, width), parts.dtype),
            pltpu.VMEM((4, lines, width), parts.dtype),
            pltpu.SemaphoreType.DMA((8,)),
            pltpu.SemaphoreType.DMA((8,)),
            pltpu.SemaphoreType.DMA((4,)),
            pltpu.SemaphoreType.DMA,
        ],
        compiler_params=pltpu.CompilerParams(
            collective_id=collective_id, has_side_effects=True, vmem_limit_bytes=40 << 20
        ),
    )(parts)


def dot(a, b, dims=((1,), (0,))):
    return lax.dot_general(a, b, (dims, ((), ())), preferred_element_type=F32)


def vmem(shape=None, index=None):
    return pl.BlockSpec(memory_space=VMEM)


def whole(*shape):
    return pl.BlockSpec(shape, lambda *_: (0,) * len(shape), pipeline_mode=pl.Buffered(1))


def side_by_side(a):
    return jnp.concatenate([a[:64], a[64:]], axis=1)


def one_below(a):
    return jnp.concatenate([a[:, :64], a[:, 64:]], axis=0)


def attend_kernel(
    tokens, gain, weights, attn_in, q_t, q_s, k_s, k_t, v_s, v_t, lse, exact, mixed
):
    scale = gain[...]

    @pl.loop(0, 8)
    def _(i):
        at = pl.ds(pl.multiple_of(i * ROWS, ROWS), ROWS)
        x = tokens[at].astype(F32)
        x = x * lax.rsqrt(jnp.mean(x * x, axis=1, keepdims=True) + EPSILON) * scale
        x = x.astype(BF16)
        attn_in[at] = x
        qkv = dot(x, weights[...]).astype(BF16).astype(F32)
        q = qkv[:, :128] * 0.125
        k, v = qkv[:, 128:192], qkv[:, 192:]
        q_s[i] = one_below(q).astype(BF16)
        q_t[i] = side_by_side(q.T).astype(BF16)
        k_s[i] = k.astype(BF16)
        v_s[i] = v.astype(BF16)
        kv_t = qkv[:, 128:].T
        k_t[i] = kv_t[:64].astype(BF16)
        v_t[i] = kv_t[64:].astype(BF16)

    key_row = lax.broadcasted_iota(jnp.int32, (ROWS, 2 * ROWS), 0)
    query_row = lax.rem(lax.broadcasted_iota(jnp.int32, (ROWS, 2 * ROWS), 1), ROWS)
    seen = key_row <= query_row

    @pl.loop(0, 8)
    def _(i):
        query = q_t[i]

        def add_block(j, carry, diagonal):
            top, total, acc = carry
            scores = dot(k_s[j], query)
            if diagonal:
                scores = jnp.where(seen, scores, -1e30)
            new_top = jnp.maximum(top, jnp.max(scores, axis=0, keepdims=True))
            fade = jnp.exp(top - new_top)
            weights = jnp.exp(scores - new_top)
            total = total * fade + jnp.sum(weights, axis=0, keepdims=True)
            acc = acc * fade + dot(v_t[j], weights.astype(BF16))
            return new_top, total, acc

        carry = (
            jnp.full((1, 2 * ROWS), -1e30, F32),
            jnp.zeros((1, 2 * ROWS), F32),
            jnp.zeros((64, 2 * ROWS), F32),
        )
        carry = lax.fori_loop(0, i, lambda j, c: add_block(j, c, False), carry)
        top, total, acc = add_block(i, carry, True)
        lse[i] = top + jnp.log(total)
        value = acc / total
        exact[i] = value
        both = jnp.concatenate([value[:, :ROWS], value[:, ROWS:]], axis=0)
        at = pl.ds(pl.multiple_of(i * ROWS, ROWS), ROWS)
        mixed[at] = both.T.astype(BF16)


def attend(tokens, gain, weights):
    shapes = [
        ((2048, 1024), BF16),
        ((8, 64, 512), BF16),
        ((8, 512, 64), BF16),
        ((8, 256, 64), BF16),
        ((8, 64, 256), BF16),
        ((8, 256, 64), BF16),
        ((8, 64, 256), BF16),
        ((8, 1, 512), F32),
        ((8, 64, 512), F32),
        ((2048, 128), BF16),
    ]
    return pl.pallas_call(
        attend_kernel,
        out_shape=[jax.ShapeDtypeStruct(s, t) for s, t in shapes],
        in_specs=[vmem()] * 3,
        out_specs=[vmem()] * len(shapes),
        compiler_params=pltpu.CompilerParams(vmem_limit_bytes=50 << 20),
    )(tokens, gain, weights)


def attend_back_kernel(
    mixed_grad, q_t, q_s, k_s, k_t, v_s, lse, exact, d, out_s, out_t, delta, dq
):
    @pl.loop(0, 8)
    def _(i):
        at = pl.ds(pl.multiple_of(i * ROWS, ROWS), ROWS)
        g = mixed_grad[at].astype(F32)
        out_s[i] = one_below(g).astype(BF16)
        g = side_by_side(g.T)
        out_t[i] = g.astype(BF16)
        delta[i] = jnp.sum(g * exact[i], axis=0, keepdims=True)
        dq[i] = jnp.zeros_like(dq[i])

    key_row = lax.broadcasted_iota(jnp.int32, (ROWS, 2 * ROWS), 0)
    query_row = lax.rem(lax.broadcasted_iota(jnp.int32, (ROWS, 2 * ROWS), 1), ROWS)
    seen = key_row <= query_row

    @pl.loop(0, 8)
    def _(j):
        key, key_t, value = k_s[j], k_t[j], v_s[j]

        def add_block(i, carry, diagonal):
            dk, dv = carry
            probs = jnp.exp(dot(key, q_t[i]) - lse[i])
            if diagonal:
                probs = jnp.where(seen, probs, 0.0)
            grad = probs * (dot(value, out_t[i]) - delta[i])
            grad = grad.astype(BF16)
            dv = dv + dot(probs.astype(BF16), out_s[i])
            dk = dk + dot(grad, q_s[i])
            dq[i] += dot(key_t, grad)
            return dk, dv

        zero = jnp.zeros((ROWS, 64), F32)
        carry = add_block(j, (zero, zero), True)
        dk, dv = lax.fori_loop(j + 1, 8, lambda i, c: add_block(i, c, False), carry)
        at = pl.ds(pl.multiple_of(j * ROWS, ROWS), ROWS)
        d[at, 128:256] = jnp.concatenate([dk, dv], axis=1).astype(BF16)

    @pl.loop(0, 8)
    def _(i):
        at = pl.ds(pl.multiple_of(i * ROWS, ROWS), ROWS)
        g = dq[i] * 0.125
        g = jnp.concatenate([g[:, :ROWS], g[:, ROWS:]], axis=0)
        d[at, 0:128] = g.T.astype(BF16)


def attend_back(mixed_grad, q_t, q_s, k_s, k_t, v_s, lse, exact):
    return pl.pallas_call(
        attend_back_kernel,
        out_shape=jax.ShapeDtypeStruct((2048, 256), BF16),
        in_specs=[vmem()] * 8,
        out_specs=vmem(),
        scratch_shapes=[
            VMEM((8, 512, 64), BF16),
            VMEM((8, 64, 512), BF16),
            VMEM((8, 1, 512), F32),
            VMEM((8, 64, 512), F32),
        ],
        compiler_params=pltpu.CompilerParams(vmem_limit_bytes=50 << 20),
    )(mixed_grad, q_t, q_s, k_s, k_t, v_s, lse, exact)


def experts_kernel(
    owner, moe, cot, routes, router, weights,
    out_parts, grad_parts, rows, slot_grads, hidden, gate_grads, up_grads,
):
    own = owner[0]
    w_gate, w_up, w_down = weights.at[0], weights.at[1], weights.at[2]
    expert = lax.broadcasted_iota(jnp.int32, (32, ROWS), 0)
    named = [[None, None] for _ in range(GROUP)]
    gates = [[None, None] for _ in range(GROUP)]
    for b in range(GROUP):
        logits = dot(router[...], moe[b], ((1,), (1,)))
        chosen = expert < 0
        for j in range(8):
            chosen = chosen | (routes[b, j : j + 1, :] == expert)
        logits = jnp.where(chosen, logits, -1e30)
        weight = jnp.where(chosen, jnp.exp(logits - jnp.max(logits, axis=0, keepdims=True)), 0.0)
        weight = weight / jnp.sum(weight, axis=0, keepdims=True)
        for k in range(2):
            mine = expert == 2 * own + k
            gates[b][k] = jnp.sum(jnp.where(mine, weight, 0.0), axis=0, keepdims=True)
            named[b][k] = jnp.sum(
                jnp.where(mine & chosen, 1.0, 0.0), axis=0, keepdims=True
            )
    before = lax.broadcasted_iota(jnp.int32, (ROWS, ROWS), 0) < lax.broadcasted_iota(
        jnp.int32, (ROWS, ROWS), 1
    )
    flat = jnp.concatenate([named[b][k] for b in range(GROUP) for k in range(2)], axis=0)
    place = dot(flat.astype(BF16), before.astype(BF16))
    slot = lax.broadcasted_iota(jnp.int32, (CAP, ROWS), 0).astype(F32)
    spread = [[None, None] for _ in range(GROUP)]
    slot_gates = [[None, None] for _ in range(GROUP)]
    for b in range(GROUP):
        for k in range(2):
            at = 2 * b + k
            hit = (slot == place[at : at + 1]) & (flat[at : at + 1] > 0.5)
            spread[b][k] = jnp.where(hit, 1.0, 0.0).astype(BF16)
            slot_gates[b][k] = jnp.sum(
                jnp.where(hit, gates[b][k], 0.0), axis=1, keepdims=True
            )
    pick = [jnp.concatenate(spread[b], axis=0) for b in range(GROUP)]
    cots = [None] * GROUP
    for b in range(GROUP):
        both = dot(pick[b], moe[b]).astype(BF16)
        rows[0, b] = both[:CAP]
        rows[1, b] = both[CAP:]
        cots[b] = dot(pick[b], cot[b])
        for k in range(2):
            slot_grads[k, b] = (slot_gates[b][k] * cots[b][k * CAP : (k + 1) * CAP]).astype(BF16)
    gated = [None, None]
    row_grads = [None, None]
    weight_grads = [None, None]
    for k in range(2):
        x = rows[k].reshape(GROUP * CAP, 1024)
        dy = slot_grads[k].reshape(GROUP * CAP, 1024)
        g = dot(x, w_gate[k])
        u = dot(x, w_up[k])
        s = jax.nn.sigmoid(g)
        silu = g * s
        h = (silu * u).astype(BF16)
        hidden[k] = h.reshape(GROUP, CAP, 512)
        y = dot(h, w_down[k], ((1,), (1,))).astype(BF16).astype(F32)
        gate = jnp.concatenate([slot_gates[b][k] for b in range(GROUP)], axis=0)
        gated[k] = (gate * y).astype(BF16)
        upstream = jnp.concatenate(
            [cots[b][k * CAP : (k + 1) * CAP] for b in range(GROUP)], axis=0
        )
        weight_grads[k] = jnp.sum(upstream * y, axis=1, keepdims=True)
        dh = dot(dy, w_down[k])
        gg = (dh * u * s * (1.0 + g * (1.0 - s))).astype(BF16)
        ug = (dh * silu).astype(BF16)
        gate_grads[k] = gg.reshape(GROUP, CAP, 512)
        up_grads[k] = ug.reshape(GROUP, CAP, 512)
        row_grads[k] = (
            dot(gg, w_gate[k], ((1,), (1,))) + dot(ug, w_up[k], ((1,), (1,)))
        ).astype(BF16)
    owner_row = lax.broadcasted_iota(jnp.int32, (16, ROWS), 0) == own
    for b in range(GROUP):
        at = slice(b * CAP, (b + 1) * CAP)
        for source, target in ((gated, out_parts), (row_grads, grad_parts)):
            both = jnp.concatenate([source[0][at], source[1][at]], axis=0)
            total = dot(pick[b], both, ((0,), (0,))).astype(BF16)
            for q in range(4):
                target[b, q, 0:ROWS] = total[:, q * 256 : (q + 1) * 256]
        for k in range(2):
            vector = jnp.sum(
                spread[b][k].astype(F32) * weight_grads[k][at], axis=0, keepdims=True
            )
            high = vector.astype(BF16)
            low = (vector - high.astype(F32)).astype(BF16)
            grad_parts[b, 2 * k, ROWS : ROWS + 16] = jnp.where(
                owner_row, high.astype(F32), 0.0
            ).astype(BF16)
            grad_parts[b, 2 * k + 1, ROWS : ROWS + 16] = jnp.where(
                owner_row, low.astype(F32), 0.0
            ).astype(BF16)


def experts(owner, moe, cot, routes, router, weights):
    steps = 16 // GROUP

    def block(*shape, dim=0):
        def index(g, owner):
            return tuple(g if i == dim else 0 for i in range(len(shape)))

        return pl.BlockSpec(shape, index)

    outs = [
        ((16, 4, 256, 256), BF16),
        ((16, 4, 272, 256), BF16),
        ((2, 16, CAP, 1024), BF16),
        ((2, 16, CAP, 1024), BF16),
        ((2, 16, CAP, 512), BF16),
        ((2, 16, CAP, 512), BF16),
        ((2, 16, CAP, 512), BF16),
    ]
    return pl.pallas_call(
        experts_kernel,
        grid_spec=pltpu.PrefetchScalarGridSpec(
            num_scalar_prefetch=1,
            grid=(steps,),
            in_specs=[
                block(GROUP, 256, 1024),
                block(GROUP, 256, 1024),
                block(GROUP, 8, 256),
                whole(32, 1024),
                whole(3, 2, 1024, 512),
            ],
            out_specs=[
                block(GROUP, 4, 256, 256),
                block(GROUP, 4, 272, 256),
                block(2, GROUP, CAP, 1024, dim=1),
                block(2, GROUP, CAP, 1024, dim=1),
                block(2, GROUP, CAP, 512, dim=1),
                block(2, GROUP, CAP, 512, dim=1),
                block(2, GROUP, CAP, 512, dim=1),
            ],
        ),
        out_shape=[jax.ShapeDtypeStruct(s, t) for s, t in outs],
        compiler_params=pltpu.CompilerParams(vmem_limit_bytes=58 << 20),
    )(owner, moe, cot, routes, router, weights)


def rms_scale(values, gain):
    return values * lax.rsqrt(jnp.mean(values * values, axis=-1, keepdims=True) + EPSILON) * gain


def per_device(
    tokens,
    norm_attn,
    w_query,
    w_key,
    w_value,
    w_out,
    norm_moe,
    w_router,
    w_gate,
    w_up,
    w_down,
    routes,
    cotangent,
):
    exp = lax.axis_index("exp")
    narrow = jnp.concatenate(
        [w_query, w_key, w_value, w_out, w_router, norm_moe[:, None], norm_attn[:, None]], axis=1
    )
    group_rows = lax.all_gather(narrow, "exp", axis=0, tiled=True)
    everyone = gather_ctx(tokens[0], 1).reshape(2048, 1024)
    by_head = jnp.concatenate(
        [
            group_rows[:, :1024].reshape(128, 8, 128),
            group_rows[:, 1024:1536].reshape(128, 8, 64),
            group_rows[:, 1536:2048].reshape(128, 8, 64),
            jnp.broadcast_to(group_rows[:, None, 3105:3106], (128, 8, 128)),
        ],
        axis=2,
    )
    by_head = lax.all_to_all(
        by_head.transpose(1, 0, 2), "ctx", split_axis=0, concat_axis=0, tiled=True
    ).reshape(1024, 384)
    head_weights = by_head[:, :256]
    gain_attn = by_head[:, 256].astype(F32)[None, :]
    wide = lax.all_gather(group_rows[:, 2048:3105], "ctx", axis=0, tiled=True)
    full_out, full_router = wide[:, :1024], wide[:, 1024:1056]
    gain_moe = wide[:, 1056].astype(F32)
    router_t = full_router.T
    all_cot = lax.all_gather(cotangent[0], "exp", axis=0, tiled=True).reshape(16, 256, 1024)
    all_routes = lax.all_gather(routes[0].T, "exp", axis=0, tiled=True).reshape(16, 8, 256)
    own_experts = jnp.stack([w_gate, w_up, w_down.transpose(0, 2, 1)]).reshape(768, 512)
    all_experts = gather_ctx(own_experts, 2).reshape(8, 3, 2, 128, 512)
    all_experts = all_experts.transpose(1, 2, 0, 3, 4).reshape(3, 2, 1024, 512)

    attn_in, q_t, q_s, k_s, k_t, v_s, v_t, lse, exact, mixed = attend(
        everyone, gain_attn, head_weights
    )
    mixed_rows = lax.all_to_all(
        mixed.reshape(8, 256, 128), "ctx", split_axis=0, concat_axis=0, tiled=True
    )
    mixed_rows = mixed_rows.transpose(1, 0, 2).reshape(256, 1024)
    token_rows = tokens[0].astype(F32)
    resid = token_rows + jnp.dot(mixed_rows, full_out, preferred_element_type=F32)
    moe_in = rms_scale(resid, gain_moe).astype(BF16)
    all_moe = gather_exp(moe_in, 3)
    out_parts, grad_parts, rows, slot_grads, hidden, gate_grads, up_grads = experts(
        exp.reshape(1).astype(jnp.int32), all_moe, all_cot, all_routes, router_t, all_experts
    )
    grad_total = reduce_exp(grad_parts, 4)
    expert_out = lax.psum_scatter(
        out_parts.reshape(-1, 256), "exp", scatter_dimension=0, tiled=True
    )
    expert_out = expert_out.reshape(4, 256, 256).transpose(1, 0, 2).reshape(256, 1024)
    output = (resid + expert_out.astype(F32)).astype(BF16)[None]

    flat = (2, 16 * CAP, -1)
    rows, slot_grads = rows.reshape(flat), slot_grads.reshape(flat)
    hidden, gate_grads, up_grads = (a.reshape(flat) for a in (hidden, gate_grads, up_grads))

    def expert_term(left, right):
        term = jnp.einsum("erd,erf->edf", left, right, preferred_element_type=F32).astype(BF16)
        return term.reshape(2, 8, 128, 512).transpose(1, 0, 2, 3)

    expert_terms = jnp.stack(
        [
            expert_term(rows, gate_grads),
            expert_term(rows, up_grads),
            expert_term(slot_grads, hidden),
        ],
        axis=1,
    ).reshape(8 * 768, 512)
    expert_sum = (
        lax.psum_scatter(expert_terms, "ctx", scatter_dimension=0, tiled=True)
        .astype(F32)
        .reshape(3, 2, 128, 512)
    )

    logits = jnp.dot(moe_in, full_router, preferred_element_type=F32)
    chosen = jnp.any(
        routes[0][:, :, None] == jnp.arange(32, dtype=jnp.int32)[None, None, :], axis=1
    )
    gates = jax.nn.softmax(jnp.where(chosen, logits, -1e30), axis=-1)
    weight_grad = (
        grad_total[:, ROWS:].astype(F32).reshape(2, 2, 16, 256).sum(axis=1)
    )
    weight_grad = weight_grad.transpose(2, 1, 0).reshape(256, 32)
    logit_grad = jnp.where(
        chosen,
        gates * (weight_grad - jnp.sum(gates * weight_grad, axis=-1, keepdims=True)),
        0.0,
    )
    router_term = jnp.dot(moe_in.astype(F32).T, logit_grad, precision=PRECISE)
    moe_in_grad = grad_total[:, :ROWS].astype(F32).transpose(1, 0, 2).reshape(256, 1024)
    moe_in_grad = moe_in_grad + jnp.dot(
        logit_grad, full_router.astype(F32).T, precision=PRECISE
    )
    unused_moe, pull_moe = jax.vjp(rms_scale, resid, gain_moe)
    resid_grad, norm_moe_term = pull_moe(moe_in_grad)
    resid_grad = resid_grad + cotangent[0].astype(F32)
    attn_grad = resid_grad.astype(BF16)
    mixed_grad = jnp.einsum(
        "td,qd->tq", attn_grad, full_out, preferred_element_type=F32
    ).astype(BF16)
    mixed_grad = lax.all_to_all(
        mixed_grad.reshape(256, 8, 128).transpose(1, 0, 2),
        "ctx",
        split_axis=0,
        concat_axis=0,
        tiled=True,
    ).reshape(2048, 128)
    all_attn_grad = gather_ctx(attn_grad, 5).reshape(2048, 1024)
    out_term = jnp.einsum("tq,td->qd", mixed, all_attn_grad, preferred_element_type=F32)
    head_grads = attend_back(mixed_grad, q_t, q_s, k_s, k_t, v_s, lse, exact)
    head_term = jnp.einsum("td,tq->dq", attn_in, head_grads, preferred_element_type=F32)
    attn_in_parts = jnp.einsum(
        "tq,dq->td", head_grads, head_weights, preferred_element_type=F32
    ).astype(BF16)
    attn_in_grad = reduce_ctx(attn_in_parts.reshape(8, 256, 1024), 6).astype(F32)

    small_term = jnp.concatenate([router_term, norm_moe_term[:, None]], axis=1)

    def by_exp(term):
        return term.reshape(-1, 16, 8, term.shape[1]).transpose(1, 0, 2, 3).reshape(16, -1)

    sums = jnp.concatenate([by_exp(head_term), by_exp(out_term), by_exp(small_term)], axis=1)
    sums = jnp.pad(sums.astype(BF16), ((0, 0), (0, 32768 - sums.shape[1])))
    sums = reduce_exp(sums.reshape(16, 4, 32, 256), 7).reshape(-1).astype(F32)
    out_sum = sums[16384:24576].reshape(8, 1024)
    spread = jnp.concatenate(
        [sums[:16384].reshape(8, 8, 256), sums[24576:26688].reshape(8, 8, 33)], axis=2
    )
    spread = lax.all_to_all(spread, "ctx", split_axis=0, concat_axis=0, tiled=True)
    small_sum = jnp.sum(spread[:, :, 256:], axis=0)
    query_sum = spread[:, :, :128].transpose(1, 0, 2).reshape(8, 1024)
    key_sum = spread[:, :, 128:192].transpose(1, 0, 2).reshape(8, 512)
    value_sum = spread[:, :, 192:256].transpose(1, 0, 2).reshape(8, 512)
    norm_attn_sum = (
        jnp.sum(query_sum * w_query.astype(F32), axis=1)
        + jnp.sum(key_sum * w_key.astype(F32), axis=1)
        + jnp.sum(value_sum * w_value.astype(F32), axis=1)
    ) / norm_attn.astype(F32)
    unused_attn, pull_attn = jax.vjp(lambda v: rms_scale(v, gain_attn), token_rows)
    (token_grad,) = pull_attn(attn_in_grad)
    token_grad = (token_grad + resid_grad).astype(BF16)[None]
    return (
        output,
        token_grad,
        norm_attn_sum,
        query_sum,
        key_sum,
        value_sum,
        out_sum,
        small_sum[:, 32],
        small_sum[:, :32],
        expert_sum[0],
        expert_sum[1],
        expert_sum[2].transpose(0, 2, 1),
    )


def solution(mesh):
    in_specs = (
        P("exp", "ctx", None),
        P(("ctx", "exp")),
        P(("ctx", "exp"), None),
        P(("ctx", "exp"), None),
        P(("ctx", "exp"), None),
        P(("ctx", "exp"), None),
        P(("ctx", "exp")),
        P(("ctx", "exp"), None),
        P("exp", "ctx", None),
        P("exp", "ctx", None),
        P("exp", None, "ctx"),
        P("exp", "ctx", None),
        P("exp", "ctx", None),
    )
    out_specs = (
        P("exp", "ctx", None),
        P("exp", "ctx", None),
        P(("ctx", "exp")),
        P(("ctx", "exp"), None),
        P(("ctx", "exp"), None),
        P(("ctx", "exp"), None),
        P(("ctx", "exp"), None),
        P(("ctx", "exp")),
        P(("ctx", "exp"), None),
        P("exp", "ctx", None),
        P("exp", "ctx", None),
        P("exp", None, "ctx"),
    )
    return jax.shard_map(
        per_device, mesh=mesh, in_specs=in_specs, out_specs=out_specs, check_vma=False
    )
```

time: 1050 us -> 504 us (0.48)
  waiting for transfers between devices: 381 us -> 3.66 us
  Pallas kernels: 0 us -> 326 us
  local copies, waits for them, and re-layouts: 259 us -> 33.4 us
  matrix products: 213 us -> 36.9 us
  other arithmetic: 104 us -> 14.2 us
  blocking collectives: 0 us -> 40.9 us
  starting transfers between devices: 60.4 us -> 27.1 us
    pallas_call x0 -> x10, Pallas kernels: none -> 326 us  [the longest x3 109 us: gather_ctx(): pl.pallas_call(gather_ctx_kernel, out_shape=jax.ShapeDtypeStruct((8,) + b...]
    all_to_all x8 -> x4, waiting for transfers between devices: 212 us -> 2.4 us  [the longest x1 2.39 us: per_device(): lax.all_to_all(mixed_grad.reshape(256, 8, 128).transpose(1, 0, 2), 'ctx',...]
    dot_general x66 -> x11, matrix products: 213 us -> 36.9 us  [the longest x3 21.3 us: expert_term(): jnp.einsum('erd,erf->edf', left, right, preferred_element_type=F32)]
    all_gather x2, waiting for transfers between devices: 97.6 us -> 0.02 us  [the longest x1 0.02 us: per_device(): wide = lax.all_gather(group_rows[:, 2048:3105], 'ctx', axis=0, tiled=True)]
    unnamed x5 -> x4, waiting for transfers between devices: 59.5 us -> 1.24 us
    all_gather x0 -> x2, blocking collectives: none -> 40.9 us  [the longest x1 21.4 us: per_device(): group_rows = lax.all_gather(narrow, 'exp', axis=0, tiled=True)]
    transpose x6 -> x7, local copies, waits for them, and re-layouts: 38.6 us -> 1.69 us  [the longest x1 1.47 us: per_device(): router_t = full_router.T]
    all_to_all x8 -> x4, starting transfers between devices: 60 us -> 27 us  [the longest x1 10.5 us: per_device(): lax.all_to_all(by_head.transpose(1, 0, 2), 'ctx', split_axis=0, concat_ax...]
  transfers between devices with their start and end apart: 12 -> 8, of which waited for: 9 -> 1; matrix products, arithmetic and copies ran while one was open for 33% -> 9% of each run, Pallas kernels for 0% -> 57%
where the time goes in v1:
time: 504 us; the launch traced here: 497 us
  Pallas kernels  326 us (65%)
  blocking collectives  40.9 us (8%)
  matrix products  36.9 us (7%)
  local copies, waits for them, and re-layouts  33.4 us (7%)
  starting transfers between devices  27.1 us (5%)
  between operations  14.7 us (3%)
  other arithmetic  14.2 us (3%)
    pallas_call x3, Pallas kernels, gather_ctx(): pl.pallas_call(gather_ctx_kernel, out_shape=jax.ShapeDtypeStruct((8,) + b...  109 us
    pallas_call x2, Pallas kernels, reduce_exp(): pl.pallas_call(reduce_exp_kernel, out_shape=jax.ShapeDtypeStruct((quarter...  60.4 us
    pallas_call x1, Pallas kernels, experts(): pl.pallas_call(experts_kernel, grid_spec=pltpu.PrefetchScalarGridSpec(num...  42.7 us
    pallas_call x1, Pallas kernels, gather_exp(): pl.pallas_call(gather_exp_kernel, out_shape=jax.ShapeDtypeStruct((16, row...  41.2 us
    pallas_call x1, Pallas kernels, attend(): pl.pallas_call(attend_kernel, out_shape=[jax.ShapeDtypeStruct(s, t) for s...  26.4 us
    pallas_call x1, Pallas kernels, reduce_ctx(): pl.pallas_call(reduce_ctx_kernel, out_shape=jax.ShapeDtypeStruct((lines,...  26.1 us
    all_gather x1, blocking collectives, per_device(): group_rows = lax.all_gather(narrow, 'exp', axis=0, tiled=True)  21.4 us
    dot_general x3, matrix products, expert_term(): jnp.einsum('erd,erf->edf', left, right, preferred_element_type=F32)  21.3 us
  transfers between devices with their start and end apart: 8, of which 1 were waited for; matrix products, arithmetic and copies ran while one was open for 9% of the time, Pallas kernels for 57%

profile of v1, /device:TPU:1, one launch (start us, length us, event | category | flops | bytes accessed | tf_op | source)
XLA Modules:
  0.0 497.3 jit_solution(1274376124104147528)
XLA Ops:
  8.7 0.8 concatenate.25
  9.6 21.4 %all_gather.12 = bf16[128,3106]{1,0:T(8,128)(2,1)S(1)} all-gather(bf16[8,3106]{1,0:T(8,128)(2,1)S(1)} %concatenate.25), channel_id=1, replica_groups=mesh['ctx'=8,'exp'=16] {'exp'}, dimensions={0}, use_global_device_ids=true | all-gather | bytes 844832 | tf_op jit(solution)/shard_map/all_gather | solution.py:726
  31.0 0.9 copy.195
  33.6 1.1 maximum_bitcast_fusion
  34.8 10.5 %all-to-all-start = ((bf16[8,128,384]{2,1,0:T(8,128)(2,1)}), bf16[8,128,384]{2,1,0:T(8,128)(2,1)S(1)}, u32[]{:S(2)}, u32[]{:S(2)}) async-start(bf16[8,128,384]{2,1,0:T(8,128)(2,1)} %maximum_bitcast_fusion), calls=%async_computation | async-start | bytes 1572864 | tf_op jit(solution)/shard_map/all_to_all | solution.py:737
  45.2 42.2 %shard_map.220 = bf16[8,256,1024]{2,1,0:T(8,128)(2,1)} custom-call(bf16[256,1024]{1,0:T(8,128)(2,1)} %bitcast.167), custom_call_target="tpu_custom_call" | custom-call | tf_op jit(solution)/shard_map/pallas_call | solution.py:307
  88.3 26.4 %shard_map.221 = (bf16[2048,1024]{1,0:T(8,128)(2,1)}, bf16[8,64,512]{2,1,0:T(8,128)(2,1)S(1)}, bf16[8,512,64]{2,1,0:T(8,128)(2,1)}, bf16[8,256,64]{2,1,0:T(8,128...) custom-call(bf16[2048,1024]{1,0:T(8,128)(2,1)} %bitcast.160, ...), custom_call_target="tpu_custom_call" | custom-call | tf_op jit(solution)/shard_map/pallas_call | solution.py:489
  114.7 1.0 copy.167
  115.8 4.1 all-to-all-start.1
  120.1 0.8 copy.170
  121.0 1.1 pad_maximum_fusion.1
  122.1 1.2 copy.171
  123.3 36.1 %shard_map.223 = bf16[8,768,512]{2,1,0:T(8,128)(2,1)} custom-call(bf16[768,512]{1,0:T(8,128)(2,1)} %bitcast.171), custom_call_target="tpu_custom_call" | custom-call | tf_op jit(solution)/shard_map/pallas_call | solution.py:307
  159.4 6.1 %copy.172 = bf16[8,3,2,128,512]{4,3,0,2,1:T(8,128)(2,1)} copy(bf16[8,3,2,128,512]{4,3,2,1,0:T(8,128)(2,1)} %bitcast.157) | data formatting | bytes 12582912 | tf_op jit(solution)/shard_map/reshape | solution.py:749
  165.5 19.5 %all_gather.15 = s32[128,256]{1,0:T(8,128)} all-gather(s32[8,256]{1,0:T(8,128)S(1)} %bitcast.197), channel_id=1, replica_groups=mesh['ctx'=8,'exp'=16] {'exp'}, dimensions={0}, use_global_device_ids=true | all-gather | bytes 139264 | tf_op jit(solution)/shard_map/all_gather | solution.py:747
  185.0 2.6 multiply_reduce_fusion.2
  188.6 0.9 multiply_convert_fusion.own
  189.6 41.2 %shard_map.222.moe = bf16[16,256,1024]{2,1,0:T(8,128)(2,1)} custom-call(bf16[256,1024]{1,0:T(8,128)(2,1)} %multiply_convert_fusion.own), custom_call_target="tpu_custom_call" | custom-call | tf_op jit(solution)/shard_map/pallas_call | solution.py:105
  230.8 1.5 slice_bitcast_fusion.1.router
  232.3 42.7 %shard_map.224 = (bf16[16,4,256,256]{3,2,1,0:T(8,128)(2,1)}, bf16[16,4,272,256]{3,2,1,0:T(8,128)(2,1)}, bf16[2,16,96,1024]{3,2,1,0:T(8,128)(2,1)}, bf16[2,16,96,...) custom-call(s32[1]{0:T(128)} %bitcast.11.owner, ...), custom_call_target="tpu_custom_call" | custom-call | tf_op jit(solution)/shard_map/pallas_call | solution.py:676
  275.0 7.3 %convolution_convert_fusion.3 = bf16[2,1024,512]{2,1,0:T(8,128)(2,1)S(1)} fusion(bf16[2,1536,1024]{2,1,0:T(8,128)(2,1)} %bitcast.203, bf16[2,1536,512]{2,1,0:T(8,128)(2,1)} %bitcast.207), kind=kOutput, calls=%fused_computation.11 | convolution fusion | flops 3222274048 | bytes 11534336 | tf_op jit(solution)/shard_map/erd,erf->edf/dot_general | solution.py:778
  282.5 6.0 %convolution_convert_fusion.2 = bf16[2,1024,512]{2,1,0:T(8,128)(2,1)S(1)} fusion(bf16[2,1536,1024]{2,1,0:T(8,128)(2,1)S(1)} %bitcast.204, bf16[2,1536,512]{2,1,0:T(8,128)(2,1)} %bitcast.206), kind=kOutput, calls=%fused_computation.10 | convolution fusion | flops 3222274048 | bytes 11534336 | tf_op jit(solution)/shard_map/erd,erf->edf/dot_general | solution.py:778
  288.5 8.0 %convolution_convert_fusion.1 = bf16[2,1024,512]{2,1,0:T(8,128)(2,1)S(1)} fusion(bf16[2,1536,1024]{2,1,0:T(8,128)(2,1)} %bitcast.202, bf16[2,1536,512]{2,1,0:T(8,128)(2,1)S(1)} %bitcast.205), kind=kOutput, calls=%fused_computation.9 | convolution fusion | flops 3222274048 | bytes 11534336 | tf_op jit(solution)/shard_map/erd,erf->edf/dot_general | solution.py:778
  296.9 3.4 pad_maximum_fusion
  301.4 1.1 fusion.35
  302.6 3.5 copy-done
  306.1 46.3 %shard_map.225 = bf16[4,272,256]{2,1,0:T(8,128)(2,1)S(1)} custom-call(bf16[16,4,272,256]{3,2,1,0:T(8,128)(2,1)S(1)} %copy-done), custom_call_target="tpu_custom_call" | custom-call | tf_op jit(solution)/shard_map/pallas_call | solution.py:222
  352.8 1.0 copy-done.2
  353.8 1.8 multiply_reduce_fusion
  355.6 1.0 copy-done.4
  356.6 1.1 fusion.32.own
  357.7 31.0 %shard_map.228 = bf16[8,256,1024]{2,1,0:T(8,128)(2,1)} custom-call(bf16[256,1024]{1,0:T(8,128)(2,1)} %fusion.32.own), custom_call_target="tpu_custom_call" | custom-call | tf_op jit(solution)/shard_map/pallas_call | solution.py:307
  388.7 2.4 fusion.12
  391.1 0.9 copy.209
  391.9 4.9 all-to-all-start.2
  396.9 3.7 convolution_convert_fusion.5
  400.6 1.8 reshape_transpose_reshape.4
  403.9 2.4 all-to-all-done.2
  406.3 20.4 %shard_map.226 = bf16[2048,256]{1,0:T(8,128)(2,1)S(1)} custom-call(bf16[2048,128]{1,0:T(8,128)(2,1)S(1)} %bitcast.153, bf16[8,64,512]{2,1,0:T(8,128)(2,1)S(1)} %get-tuple-element.31.q_t, bf16[8,512,64]{2,1,0:T(8,128)(2,1)} %get-tuple-element.32.q_s, bf16[8,256,64]{2,1,0:T(8,128)(2,1)S(1)} %get-tuple-element.33.k_s, ...), custom_call_target="tpu_custom_call" | custom-call | tf_op jit(solution)/shard_map/pallas_call | solution.py:546
  426.8 1.3 convolution_convert_fusion.4
  428.7 14.1 %shard_map.229 = bf16[4,32,256]{2,1,0:T(8,128)(2,1)S(1)} custom-call(bf16[16,4,32,256]{3,2,1,0:T(8,128)(2,1)S(1)} %bitcast.151), custom_call_target="tpu_custom_call" | custom-call | tf_op jit(solution)/shard_map/pallas_call | solution.py:222
  443.7 7.5 %all-to-all-start.3 = ((f32[8,8,289]{2,1,0:T(8,128)}), f32[8,8,289]{2,1,0:T(8,128)S(1)}, u32[]{:S(2)}, u32[]{:S(2)}) async-start(f32[8,8,289]{2,1,0:T(8,128)} %maximum_convert_fusion), calls=%async_computation.4 | async-start | bytes 196608 | tf_op jit(solution)/shard_map/all_to_all | solution.py:849
  451.2 2.3 convolution_convert_fusion
  453.6 26.1 %shard_map.227 = bf16[256,1024]{1,0:T(8,128)(2,1)S(1)} custom-call(bf16[8,256,1024]{2,1,0:T(8,128)(2,1)S(1)} %bitcast.150), custom_call_target="tpu_custom_call" | custom-call | tf_op jit(solution)/shard_map/pallas_call | solution.py:378
  483.1 2.3 fusion.34
  485.4 2.2 copy.189
  487.6 1.2 convert_bitcast_fusion
  489.0 1.6 fusion.23
  (125 shorter events, 13.9 us)
Async XLA Ops:
  7.2 177.8 %all-gather.4.cloned.1.call-start = ((), (), s32[]{:S(2)}) async-start(), calls=%async_computation.6 | async-start | bytes 2451456 | tf_op jit(solution)/shard_map/all_gather | solution.py:742
  31.9 200.4 %all-gather.6.cloned.1.call-start = ((), (), s32[]{:S(2)}) async-start(), calls=%async_computation.9 | async-start | bytes 8912896 | tf_op jit(solution)/shard_map/all_gather | solution.py:746
  34.8 52.6 %all-to-all-start = ((bf16[8,128,384]{2,1,0:T(8,128)(2,1)}), bf16[8,128,384]{2,1,0:T(8,128)(2,1)S(1)}, u32[]{:S(2)}, u32[]{:S(2)}) async-start(bf16[8,128,384]{2,1,0:T(8,128)(2,1)} %maximum_bitcast_fusion), calls=%async_computation | async-start | bytes 1572864 | tf_op jit(solution)/shard_map/all_to_all | solution.py:737
  87.4 0.9 copy-start.8
  88.3 31.6 %copy-start.15 = (bf16[2,128,512]{2,1,0:T(8,128)(2,1)S(1)}, bf16[2,128,512]{2,1,0:T(8,128)(2,1)}, u32[]{:S(2)}) copy-start(bf16[2,128,512]{2,1,0:T(8,128)(2,1)} %param.21) | copy-start | bytes 786436
  88.3 31.8 %copy-start.16 = (bf16[2,128,512]{2,1,0:T(8,128)(2,1)S(1)}, bf16[2,128,512]{2,1,0:T(8,128)(2,1)}, u32[]{:S(2)}) copy-start(bf16[2,128,512]{2,1,0:T(8,128)(2,1)} %param.22) | copy-start | bytes 786436
  115.8 69.2 %all-to-all-start.1 = ((bf16[8,256,128]{1,2,0:T(8,128)(2,1)}), bf16[8,256,128]{1,2,0:T(8,128)(2,1)}, u32[]{:S(2)}, u32[]{:S(2)}) async-start(bf16[8,256,128]{1,2,0:T(8,128)(2,1)} %copy.167), calls=%async_computation.1 | async-start | bytes 1048576 | tf_op jit(solution)/shard_map/all_to_all | solution.py:755
  119.9 363.2 %reduce-scatter.5.cloned.1.call-start = ((), (), s32[]{:S(2)}) async-start(), calls=%async_computation.8 | async-start | bytes 7077888 | tf_op jit(solution)/shard_map/reduce_scatter | solution.py:790
  159.4 6.2 %copy-start.20 = (s32[1,256,8]{1,2,0:T(8,128)S(1)}, s32[1,256,8]{1,2,0:T(8,128)}, u32[]{:S(2)}) copy-start(s32[1,256,8]{1,2,0:T(8,128)} %param.24) | copy-start | bytes 24580
  159.4 25.7 %copy-start.9 = (bf16[1,256,1024]{2,1,0:T(8,128)(2,1)S(1)}, bf16[1,256,1024]{2,1,0:T(8,128)(2,1)}, u32[]{:S(2)}) copy-start(bf16[1,256,1024]{2,1,0:T(8,128)(2,1)} %param.13) | copy-start | bytes 1572868
  187.7 1.0 copy-start.1
  275.0 7.5 %copy-start.25 = (bf16[2,16,96,1024]{3,2,1,0:T(8,128)(2,1)S(1)}, bf16[2,16,96,1024]{3,2,1,0:T(8,128)(2,1)}, u32[]{:S(2)}) copy-start(bf16[2,16,96,1024]{3,2,1,0:T(8,128)(2,1)} %get-tuple-element.39) | copy-start | bytes 18874372
  282.5 6.0 %copy-start.27 = (bf16[2,16,96,512]{3,2,1,0:T(8,128)(2,1)S(1)}, bf16[2,16,96,512]{3,2,1,0:T(8,128)(2,1)}, u32[]{:S(2)}) copy-start(bf16[2,16,96,512]{3,2,1,0:T(8,128)(2,1)} %get-tuple-element.43) | copy-start | bytes 9437188
  300.3 187.2 %reduce-scatter.3.cloned.1.call-start = ((), (), s32[]{:S(2)}) async-start(), calls=%async_computation.7 | async-start | bytes 8912896 | tf_op jit(solution)/shard_map/reduce_scatter | solution.py:767
  300.4 1.0 copy-start.6
  302.6 3.5 copy-start
  352.5 1.2 copy-start.2
  352.6 4.0 copy-start.11
  355.6 1.0 copy-start.4
  357.7 31.0 %copy-start.13 = (bf16[256,1024]{1,0:T(8,128)(2,1)S(1)}, bf16[256,1024]{1,0:T(8,128)(2,1)}, u32[]{:S(2)}) copy-start(bf16[256,1024]{1,0:T(8,128)(2,1)} %fusion.32.own) | copy-start | bytes 1572868
  391.9 10.4 %copy-start.7 = (bf16[256,1024]{1,0:T(8,128)(2,1)S(1)}, bf16[256,1024]{1,0:T(8,128)(2,1)}, u32[]{:S(2)}) copy-start(bf16[256,1024]{1,0:T(8,128)(2,1)} %multiply_convert_fusion.own) | copy-start | bytes 1572868
  391.9 14.3 %all-to-all-start.2 = ((bf16[8,256,128]{2,1,0:T(8,128)(2,1)}), bf16[8,256,128]{2,1,0:T(8,128)(2,1)S(1)}, u32[]{:S(2)}, u32[]{:S(2)}) async-start(bf16[8,256,128]{2,1,0:T(8,128)(2,1)} %bitcast.173), calls=%async_computation.3 | async-start | bytes 1048576 | tf_op jit(solution)/shard_map/all_to_all | solution.py:821
  406.3 20.5 %copy-start.26 = (bf16[2048,1024]{1,0:T(8,128)(2,1)S(1)}, bf16[2048,1024]{1,0:T(8,128)(2,1)}, u32[]{:S(2)}) copy-start(bf16[2048,1024]{1,0:T(8,128)(2,1)} %get-tuple-element.38) | copy-start | bytes 12582916
  426.8 1.7 copy-start.14
  443.7 37.0 %all-to-all-start.3 = ((f32[8,8,289]{2,1,0:T(8,128)}), f32[8,8,289]{2,1,0:T(8,128)S(1)}, u32[]{:S(2)}, u32[]{:S(2)}) async-start(f32[8,8,289]{2,1,0:T(8,128)} %maximum_convert_fusion), calls=%async_computation.4 | async-start | bytes 196608 | tf_op jit(solution)/shard_map/all_to_all | solution.py:849
  453.5 26.1 %copy-start.10 = (bf16[1,256,1024]{2,1,0:T(8,128)(2,1)S(1)}, bf16[1,256,1024]{2,1,0:T(8,128)(2,1)}, u32[]{:S(2)}) copy-start(bf16[1,256,1024]{2,1,0:T(8,128)(2,1)} %param.13) | copy-start | bytes 1572868
  453.5 28.1 %copy-start.21 = (bf16[8,512]{1,0:T(8,128)(2,1)S(1)}, bf16[8,512]{1,0:T(8,128)(2,1)}, u32[]{:S(2)}) copy-start(bf16[8,512]{1,0:T(8,128)(2,1)} %param.16) | copy-start | bytes 24580
  453.6 28.1 %copy-start.22 = (bf16[8,512]{1,0:T(8,128)(2,1)S(1)}, bf16[8,512]{1,0:T(8,128)(2,1)}, u32[]{:S(2)}) copy-start(bf16[8,512]{1,0:T(8,128)(2,1)} %param.17) | copy-start | bytes 24580
  453.6 28.2 %copy-start.19 = (bf16[8,1024]{1,0:T(8,128)(2,1)S(1)}, bf16[8,1024]{1,0:T(8,128)(2,1)}, u32[]{:S(2)}) copy-start(bf16[8,1024]{1,0:T(8,128)(2,1)} %param.15) | copy-start | bytes 49156
  453.6 29.0 %copy-start.24 = (bf16[8]{0:T(256)(128)(2,1)S(1)}, bf16[8]{0:T(256)(128)(2,1)}, u32[]{:S(2)}) copy-start(bf16[8]{0:T(256)(128)(2,1)} %param.14) | copy-start | bytes 52
  480.9 8.0 %copy-start.17 = (f32[8,512]{1,0:T(8,128)}, f32[8,512]{1,0:T(8,128)S(1)}, u32[]{:S(2)}) copy-start(f32[8,512]{1,0:T(8,128)S(1)} %reshape.274) | copy-start | bytes 49156
  480.9 8.0 %copy-start.18 = (f32[8,512]{1,0:T(8,128)}, f32[8,512]{1,0:T(8,128)S(1)}, u32[]{:S(2)}) copy-start(f32[8,512]{1,0:T(8,128)S(1)} %reshape.275) | copy-start | bytes 49156
  481.0 8.0 %copy-start.23 = (f32[8,33]{1,0:T(8,128)}, f32[8,33]{1,0:T(8,128)S(1)}, u32[]{:S(2)}) copy-start(f32[8,33]{1,0:T(8,128)S(1)} %slice_reduce_fusion) | copy-start | bytes 3172
  485.4 3.5 copy-start.3
  485.4 3.5 copy-start.5
  487.6 1.4 copy-start.12
Sparse Core Ops, SparseCore 0:
  32.0 44.5 all-gather.3
  78.8 71.4 all-gather.5
  300.5 45.9 reduce-scatter.4
  349.7 84.3 reduce-scatter.2

commit v2 on v1

--- a/solution.py
+++ b/solution.py
@@ -559,19 +559,25 @@
 
 
 def experts_kernel(
-    owner, moe, cot, routes, router, weights,
+    owner, moe, cot, routes, misc, weights,
     out_parts, grad_parts, rows, slot_grads, hidden, gate_grads, up_grads,
 ):
     own = owner[0]
-    w_gate, w_up, w_down = weights.at[0], weights.at[1], weights.at[2]
+    router = misc[0:32].astype(BF16)
+    listed = [routes[b].astype(jnp.int32) for b in range(GROUP)]
+    listed = [jnp.concatenate([r[:8], r[8:]], axis=1) for r in listed]
+
+    def matrix(kind, k):
+        return weights[:, 2 * kind + k].reshape(1024, 512)
+
     expert = lax.broadcasted_iota(jnp.int32, (32, ROWS), 0)
     named = [[None, None] for _ in range(GROUP)]
     gates = [[None, None] for _ in range(GROUP)]
     for b in range(GROUP):
-        logits = dot(router[...], moe[b], ((1,), (1,)))
+        logits = dot(router, moe[b], ((1,), (1,)))
         chosen = expert < 0
         for j in range(8):
-            chosen = chosen | (routes[b, j : j + 1, :] == expert)
+            chosen = chosen | (listed[b][j : j + 1] == expert)
         logits = jnp.where(chosen, logits, -1e30)
         weight = jnp.where(chosen, jnp.exp(logits - jnp.max(logits, axis=0, keepdims=True)), 0.0)
         weight = weight / jnp.sum(weight, axis=0, keepdims=True)
@@ -612,26 +618,26 @@
     for k in range(2):
         x = rows[k].reshape(GROUP * CAP, 1024)
         dy = slot_grads[k].reshape(GROUP * CAP, 1024)
-        g = dot(x, w_gate[k])
-        u = dot(x, w_up[k])
+        g = dot(x, matrix(0, k))
+        u = dot(x, matrix(1, k))
         s = jax.nn.sigmoid(g)
         silu = g * s
         h = (silu * u).astype(BF16)
         hidden[k] = h.reshape(GROUP, CAP, 512)
-        y = dot(h, w_down[k], ((1,), (1,))).astype(BF16).astype(F32)
+        y = dot(h, matrix(2, k), ((1,), (1,))).astype(BF16).astype(F32)
         gate = jnp.concatenate([slot_gates[b][k] for b in range(GROUP)], axis=0)
         gated[k] = (gate * y).astype(BF16)
         upstream = jnp.concatenate(
             [cots[b][k * CAP : (k + 1) * CAP] for b in range(GROUP)], axis=0
         )
         weight_grads[k] = jnp.sum(upstream * y, axis=1, keepdims=True)
-        dh = dot(dy, w_down[k])
+        dh = dot(dy, matrix(2, k))
         gg = (dh * u * s * (1.0 + g * (1.0 - s))).astype(BF16)
         ug = (dh * silu).astype(BF16)
         gate_grads[k] = gg.reshape(GROUP, CAP, 512)
         up_grads[k] = ug.reshape(GROUP, CAP, 512)
         row_grads[k] = (
-            dot(gg, w_gate[k], ((1,), (1,))) + dot(ug, w_up[k], ((1,), (1,)))
+            dot(gg, matrix(0, k), ((1,), (1,))) + dot(ug, matrix(1, k), ((1,), (1,)))
         ).astype(BF16)
     owner_row = lax.broadcasted_iota(jnp.int32, (16, ROWS), 0) == own
     for b in range(GROUP):
@@ -655,7 +661,7 @@
             ).astype(BF16)
 
 
-def experts(owner, moe, cot, routes, router, weights):
+def experts(owner, moe, cot, routes, misc, weights):
     steps = 16 // GROUP
 
     def block(*shape, dim=0):
@@ -681,9 +687,9 @@
             in_specs=[
                 block(GROUP, 256, 1024),
                 block(GROUP, 256, 1024),
-                block(GROUP, 8, 256),
-                whole(32, 1024),
-                whole(3, 2, 1024, 512),
+                block(GROUP, 16, 128),
+                whole(40, 1024),
+                whole(8, 6, 128, 512),
             ],
             out_specs=[
                 block(GROUP, 4, 256, 256),
@@ -697,7 +703,391 @@
         ),
         out_shape=[jax.ShapeDtypeStruct(s, t) for s, t in outs],
         compiler_params=pltpu.CompilerParams(vmem_limit_bytes=58 << 20),
-    )(owner, moe, cot, routes, router, weights)
+    )(owner, moe, cot, routes, misc, weights)
+
+PEERS = ((2, False), (2, True), (1, False), (1, True), (-1, False), (-1, True), (0, True))
+
+
+def greet(ctx_peers, exp_steps):
+    barrier = pltpu.get_barrier_semaphore()
+    for step, other in ctx_peers:
+        pl.semaphore_signal(
+            barrier, inc=1, device_id={"ctx": ctx_block(step, other)}, device_id_type=MESH
+        )
+    for first, second in exp_steps:
+        pl.semaphore_signal(
+            barrier, inc=1, device_id={"exp": exp_block(first, second, 0, 0)}, device_id_type=MESH
+        )
+    pl.semaphore_wait(barrier, len(ctx_peers) + len(exp_steps))
+
+
+NEIGHBOURS = ((1, 0), (-1, 0), (0, 1), (0, -1))
+
+
+def to_ctx(src, dst, send, recv, peer):
+    return pltpu.make_async_remote_copy(
+        src_ref=src,
+        dst_ref=dst,
+        send_sem=send,
+        recv_sem=recv,
+        device_id={"ctx": ctx_block(*peer)},
+        device_id_type=MESH,
+    )
+
+
+def gather_exp_stages(own, out, send, recv):
+    rows = own.shape[0]
+    copies = {
+        (half, axis, k, s): gather_exp_copy(own, out, send, recv, rows, half, axis, k, s)
+        for half in range(2)
+        for axis, k in ((1, 0), (2, 0), (2, 1), (2, -1), (2, 2))
+        for s in range(4)
+    }
+
+    def begin():
+        for axis in (1, 2):
+            for s in (0, 1):
+                for half in range(2):
+                    copies[half, axis, 0, s].start()
+
+    def first(s, k):
+        for half in range(2):
+            copies[half, 1, 0, s].wait_recv()
+            copies[half, 1, 0, s + 2].start()
+            copies[half, 2, k, 0].start()
+            copies[half, 2, k, 1].start()
+
+    def middle():
+        for half in range(2):
+            copies[half, 1, 0, 2].wait_recv()
+            copies[half, 1, 0, 3].wait_recv()
+            copies[half, 2, 2, 0].start()
+            copies[half, 2, 2, 1].start()
+
+    def forward(k):
+        for s in (0, 1):
+            for half in range(2):
+                copies[half, 2, k, s].wait_recv()
+                copies[half, 2, k, s + 2].start()
+
+    def last():
+        for k in (0, -1, 1, 2):
+            for s in (2, 3):
+                for half in range(2):
+                    copies[half, 2, k, s].wait_recv()
+
+    def sent():
+        for copy in copies.values():
+            copy.wait_send()
+
+    steps = [
+        begin,
+        lambda: first(0, -1),
+        lambda: first(1, 1),
+        lambda: forward(0),
+        middle,
+        lambda: forward(-1),
+        lambda: forward(1),
+        lambda: forward(2),
+        last,
+    ]
+    return steps, sent
+
+
+def start_kernel(
+    tokens, cot, w_gate, w_up, w_down, pieces, out_piece, routes,
+    attn_in, q_t, q_s, k_s, k_t, v_s, lse, exact, mixed,
+    head_w, misc_t, full_out, resid, moe_in, all_cot, all_routes, all_experts,
+    land, own_experts, down_in, w_block, w_all, o_block, o_all, w_wide, o_wide, misc, v_t, mixed_land,
+    exp_send, exp_recv, ctx_send, ctx_recv, ring_send, ring_recv, local,
+):
+    me = lax.axis_index("ctx")
+    own = exp_block(0, 0, 0, 0)
+    loads = [
+        pltpu.make_async_copy(w_gate, own_experts.at[pl.ds(0, 2)], local.at[0]),
+        pltpu.make_async_copy(w_up, own_experts.at[pl.ds(2, 2)], local.at[1]),
+        pltpu.make_async_copy(w_down, down_in, local.at[2]),
+        pltpu.make_async_copy(tokens, land.at[me], local.at[3]),
+        pltpu.make_async_copy(pieces.at[me], w_block.at[pl.ds(me * 32, 32)], local.at[4]),
+        pltpu.make_async_copy(routes, w_block.at[pl.ds(256, 64)], local.at[5]),
+        pltpu.make_async_copy(out_piece, o_block.at[pl.ds(me * 64, 64)], local.at[6]),
+        pltpu.make_async_copy(cot, all_cot.at[own], local.at[7]),
+    ]
+    for load in loads:
+        load.start()
+    greet(PEERS, NEIGHBOURS)
+    piece_copies = [
+        to_ctx(
+            pieces.at[ctx_block(*peer)], w_block.at[pl.ds(me * 32, 32)],
+            ctx_send.at[0, at], ctx_recv.at[0, at], peer,
+        )
+        for at, peer in enumerate(PEERS)
+    ]
+    out_copies = [
+        to_ctx(
+            out_piece, o_block.at[pl.ds(me * 64, 64)],
+            ctx_send.at[1, at], ctx_recv.at[1, at], peer,
+        )
+        for at, peer in enumerate(PEERS)
+    ]
+    for copy in piece_copies + out_copies:
+        copy.start()
+    ring = gather_ctx_copies(tokens, land, ring_send.at[0], ring_recv.at[0])
+    for at in (1, 2, 0):
+        ring[at].start()
+    w_steps, w_sent = gather_exp_stages(w_block, w_all, exp_send.at[0], exp_recv.at[0])
+    o_steps, o_sent = gather_exp_stages(o_block, o_all, exp_send.at[1], exp_recv.at[1])
+    c_steps, c_sent = gather_exp_stages(cot, all_cot, exp_send.at[2], exp_recv.at[2])
+    for copy in piece_copies:
+        copy.wait_recv()
+    loads[4].wait()
+    loads[5].wait()
+    w_steps[0]()
+    w_keep = pltpu.make_async_copy(w_block, w_all.at[own], local.at[8])
+    w_keep.start()
+    for copy in out_copies:
+        copy.wait_recv()
+    loads[6].wait()
+    o_steps[0]()
+    o_keep = pltpu.make_async_copy(o_block, o_all.at[own], local.at[9])
+    o_keep.start()
+    c_steps[0]()
+    for at in (0, 1, 2):
+        loads[at].wait()
+    for k in range(2):
+        own_experts[4 + k] = down_in[k].astype(F32).T.astype(BF16)
+    for step in w_steps[1:]:
+        step()
+    w_keep.wait()
+    ring[1].wait_recv()
+    ring[3].start()
+    ring[5].start()
+    ring[2].wait_recv()
+    ring[4].start()
+    ring[6].start()
+
+    @pl.loop(0, 128)
+    def _(i):
+        x, c = lax.div(i, 8), lax.rem(i, 8)
+        at = pl.ds(pl.multiple_of(c * 128 + x * 8, 8), 8)
+        line = pl.multiple_of(c * 32, 32)
+        first = w_all[x, pl.ds(line, 16)].astype(F32)
+        second = w_all[x, pl.ds(line + 16, 16)].astype(F32)
+        w_wide[at, 0:128] = first[:8]
+        w_wide[at, 128:256] = first[8:]
+        misc[at] = second[:8]
+
+    all_routes[...] = w_all[:, 256:272]
+    head_w[...] = w_wide[...].astype(BF16)
+
+    @pl.loop(0, 8)
+    def _(c):
+        at = pl.ds(pl.multiple_of(c * 128, 128), 128)
+        misc_t[:, at] = misc[at].T[:40]
+
+    def project(i):
+        at = pl.ds(pl.multiple_of(i * ROWS, ROWS), ROWS)
+        x = land[i].astype(F32)
+        x = x * lax.rsqrt(jnp.mean(x * x, axis=1, keepdims=True) + EPSILON) * misc_t[33:34]
+        x = x.astype(BF16)
+        attn_in[at] = x
+        qkv = dot(x, head_w[...]).astype(BF16).astype(F32)
+        q = qkv[:, :128] * 0.125
+        k, v = qkv[:, 128:192], qkv[:, 192:]
+        q_s[i] = one_below(q).astype(BF16)
+        q_t[i] = side_by_side(q.T).astype(BF16)
+        k_s[i] = k.astype(BF16)
+        v_s[i] = v.astype(BF16)
+        kv_t = qkv[:, 128:].T
+        k_t[i] = kv_t[:64].astype(BF16)
+        v_t[i] = kv_t[64:].astype(BF16)
+
+    o_steps[1]()
+    o_steps[2]()
+    loads[3].wait()
+    project(ctx_block(0, False))
+    ring[0].wait_recv()
+    project(ctx_block(0, True))
+    ring[3].wait_recv()
+    ring[7].start()
+    ring[4].wait_recv()
+    ring[8].start()
+    w_ring = gather_ctx_copies(own_experts, all_experts, ring_send.at[1], ring_recv.at[1])
+    for at in (1, 2, 0):
+        w_ring[at].start()
+    w_ring_keep = pltpu.make_async_copy(own_experts, all_experts.at[me], local.at[10])
+    w_ring_keep.start()
+    o_steps[3]()
+    o_steps[4]()
+    c_steps[1]()
+    c_steps[2]()
+    project(ctx_block(-1, False))
+    project(ctx_block(1, False))
+    ring[5].wait_recv()
+    project(ctx_block(-1, True))
+    ring[6].wait_recv()
+    project(ctx_block(1, True))
+    project(ctx_block(2, False))
+    ring[7].wait_recv()
+    ring[8].wait_recv()
+    project(ctx_block(2, True))
+
+    key_row = lax.broadcasted_iota(jnp.int32, (ROWS, 2 * ROWS), 0)
+    query_row = lax.rem(lax.broadcasted_iota(jnp.int32, (ROWS, 2 * ROWS), 1), ROWS)
+    seen = key_row <= query_row
+
+    def tile(i):
+        query = q_t[i]
+
+        def add_block(j, carry, diagonal):
+            top, total, acc = carry
+            scores = dot(k_s[j], query)
+            if diagonal:
+                scores = jnp.where(seen, scores, -1e30)
+            new_top = jnp.maximum(top, jnp.max(scores, axis=0, keepdims=True))
+            fade = jnp.exp(top - new_top)
+            weights = jnp.exp(scores - new_top)
+            total = total * fade + jnp.sum(weights, axis=0, keepdims=True)
+            acc = acc * fade + dot(v_t[j], weights.astype(BF16))
+            return new_top, total, acc
+
+        carry = (
+            jnp.full((1, 2 * ROWS), -1e30, F32),
+            jnp.zeros((1, 2 * ROWS), F32),
+            jnp.zeros((64, 2 * ROWS), F32),
+        )
+        carry = lax.fori_loop(0, i, lambda j, c: add_block(j, c, False), carry)
+        top, total, acc = add_block(i, carry, True)
+        lse[i] = top + jnp.log(total)
+        value = acc / total
+        exact[i] = value
+        both = jnp.concatenate([value[:, :ROWS], value[:, ROWS:]], axis=0)
+        mixed[i] = both.T.astype(BF16)
+
+    def unpack_out():
+        o_keep.wait()
+
+        @pl.loop(0, 128)
+        def _(i):
+            x, c = lax.div(i, 8), lax.rem(i, 8)
+            at = pl.ds(pl.multiple_of(c * 128 + x * 8, 8), 8)
+            for t in range(4):
+                line = pl.multiple_of(c * 64 + t * 16, 16)
+                both = o_all[x, pl.ds(line, 16)].astype(F32)
+                o_wide[at, 256 * t : 256 * t + 128] = both[:8]
+                o_wide[at, 256 * t + 128 : 256 * t + 256] = both[8:]
+
+        full_out[...] = o_wide[...].astype(BF16)
+
+    def ring_first():
+        w_ring[1].wait_recv()
+        w_ring[3].start()
+        w_ring[5].start()
+        w_ring[2].wait_recv()
+        w_ring[4].start()
+        w_ring[6].start()
+
+    def ring_second():
+        w_ring[3].wait_recv()
+        w_ring[7].start()
+        w_ring[4].wait_recv()
+        w_ring[8].start()
+
+    between = (
+        (o_steps[5], o_steps[6]),
+        (o_steps[7], c_steps[3]),
+        (c_steps[4], ring_first),
+        (c_steps[5], o_steps[8]),
+        (unpack_out,),
+        (c_steps[6],),
+        (c_steps[7], ring_second),
+    )
+    mixed_copies = []
+    for at, peer in enumerate(PEERS):
+        i = ctx_block(*peer)
+        tile(i)
+        copy = to_ctx(
+            mixed.at[i], mixed_land.at[me], ctx_send.at[2, at], ctx_recv.at[2, at], peer
+        )
+        copy.start()
+        mixed_copies.append(copy)
+        for step in between[at]:
+            step()
+    tile(me)
+    mixed_land[me] = mixed[me]
+    total = tokens[...].astype(F32)
+    for copy in mixed_copies:
+        copy.wait_recv()
+    for c in range(4):
+        pair = jnp.concatenate([mixed_land[2 * c], mixed_land[2 * c + 1]], axis=1)
+        total = total + dot(pair, full_out[c * 256 : (c + 1) * 256])
+    resid[...] = total
+    scaled = total * lax.rsqrt(jnp.mean(total * total, axis=1, keepdims=True) + EPSILON)
+    moe_in[...] = (scaled * misc_t[32:33]).astype(BF16)
+    c_steps[8]()
+    for at in (0, 5, 6, 7, 8):
+        w_ring[at].wait_recv()
+    w_ring_keep.wait()
+    loads[7].wait()
+    w_sent()
+    o_sent()
+    c_sent()
+    for copy in (*piece_copies, *out_copies, *ring, *w_ring, *mixed_copies):
+        copy.wait_send()
+
+
+def start(tokens, cot, w_gate, w_up, w_down, pieces, out_piece, routes, collective_id):
+    anywhere = pl.BlockSpec(memory_space=pl.ANY)
+    outs = [
+        ((2048, 1024), BF16, vmem()),
+        ((8, 64, 512), BF16, vmem()),
+        ((8, 512, 64), BF16, vmem()),
+        ((8, 256, 64), BF16, vmem()),
+        ((8, 64, 256), BF16, vmem()),
+        ((8, 256, 64), BF16, vmem()),
+        ((8, 1, 512), F32, vmem()),
+        ((8, 64, 512), F32, vmem()),
+        ((8, 256, 128), BF16, vmem()),
+        ((1024, 256), BF16, vmem()),
+        ((40, 1024), F32, vmem()),
+        ((1024, 1024), BF16, vmem()),
+        ((256, 1024), F32, vmem()),
+        ((256, 1024), BF16, vmem()),
+        ((16, 256, 1024), BF16, anywhere),
+        ((16, 16, 128), BF16, vmem()),
+        ((8, 6, 128, 512), BF16, anywhere),
+    ]
+    dma = pltpu.SemaphoreType.DMA
+    return pl.pallas_call(
+        start_kernel,
+        out_shape=[jax.ShapeDtypeStruct(s, t) for s, t, _ in outs],
+        in_specs=[vmem(), anywhere, anywhere, anywhere, anywhere, vmem(), vmem(), vmem()],
+        out_specs=[spec for _, _, spec in outs],
+        scratch_shapes=[
+            VMEM((8, 256, 1024), BF16),
+            VMEM((6, 128, 512), BF16),
+            VMEM((2, 512, 128), BF16),
+            VMEM((320, 128), BF16),
+            VMEM((16, 320, 128), BF16),
+            VMEM((512, 128), BF16),
+            VMEM((16, 512, 128), BF16),
+            VMEM((1024, 256), F32),
+            VMEM((1024, 1024), F32),
+            VMEM((1024, 128), F32),
+            VMEM((8, 64, 256), BF16),
+            VMEM((8, 256, 128), BF16),
+            dma((3, 40)),
+            dma((3, 40)),
+            dma((3, 7)),
+            dma((3, 7)),
+            dma((2, 9)),
+            dma((2, 9)),
+            dma((11,)),
+        ],
+        compiler_params=pltpu.CompilerParams(
+            collective_id=collective_id, has_side_effects=True, vmem_limit_bytes=56 << 20
+        ),
+    )(tokens, cot, w_gate, w_up, w_down, pieces, out_piece, routes)
 
 
 def rms_scale(values, gain):
@@ -720,48 +1110,30 @@
     cotangent,
 ):
     exp = lax.axis_index("exp")
-    narrow = jnp.concatenate(
-        [w_query, w_key, w_value, w_out, w_router, norm_moe[:, None], norm_attn[:, None]], axis=1
-    )
-    group_rows = lax.all_gather(narrow, "exp", axis=0, tiled=True)
-    everyone = gather_ctx(tokens[0], 1).reshape(2048, 1024)
     by_head = jnp.concatenate(
-        [
-            group_rows[:, :1024].reshape(128, 8, 128),
-            group_rows[:, 1024:1536].reshape(128, 8, 64),
-            group_rows[:, 1536:2048].reshape(128, 8, 64),
-            jnp.broadcast_to(group_rows[:, None, 3105:3106], (128, 8, 128)),
-        ],
-        axis=2,
-    )
-    by_head = lax.all_to_all(
-        by_head.transpose(1, 0, 2), "ctx", split_axis=0, concat_axis=0, tiled=True
-    ).reshape(1024, 384)
-    head_weights = by_head[:, :256]
-    gain_attn = by_head[:, 256].astype(F32)[None, :]
-    wide = lax.all_gather(group_rows[:, 2048:3105], "ctx", axis=0, tiled=True)
-    full_out, full_router = wide[:, :1024], wide[:, 1024:1056]
-    gain_moe = wide[:, 1056].astype(F32)
-    router_t = full_router.T
-    all_cot = lax.all_gather(cotangent[0], "exp", axis=0, tiled=True).reshape(16, 256, 1024)
-    all_routes = lax.all_gather(routes[0].T, "exp", axis=0, tiled=True).reshape(16, 8, 256)
-    own_experts = jnp.stack([w_gate, w_up, w_down.transpose(0, 2, 1)]).reshape(768, 512)
-    all_experts = gather_ctx(own_experts, 2).reshape(8, 3, 2, 128, 512)
-    all_experts = all_experts.transpose(1, 2, 0, 3, 4).reshape(3, 2, 1024, 512)
-
-    attn_in, q_t, q_s, k_s, k_t, v_s, v_t, lse, exact, mixed = attend(
-        everyone, gain_attn, head_weights
-    )
-    mixed_rows = lax.all_to_all(
-        mixed.reshape(8, 256, 128), "ctx", split_axis=0, concat_axis=0, tiled=True
-    )
-    mixed_rows = mixed_rows.transpose(1, 0, 2).reshape(256, 1024)
+        [w_query.reshape(8, 8, 128), w_key.reshape(8, 8, 64), w_value.reshape(8, 8, 64)], axis=2
+    ).transpose(1, 0, 2)
+    narrow = jnp.concatenate([w_router, norm_moe[:, None], norm_attn[:, None]], axis=1)
+    narrow = jnp.broadcast_to(jnp.pad(narrow, ((0, 0), (0, 94))), (8, 8, 128))
+    pieces = jnp.concatenate(
+        [by_head[:, :, :128], by_head[:, :, 128:], narrow, jnp.zeros_like(narrow)], axis=1
+    )
+    out_piece = w_out.reshape(8, 8, 128).transpose(1, 0, 2).reshape(64, 128)
+    route_rows = routes[0].T.reshape(8, 2, 128).transpose(1, 0, 2).reshape(16, 128)
+    route_rows = jnp.pad(route_rows.astype(BF16), ((0, 48), (0, 0)))
+    (
+        attn_in, q_t, q_s, k_s, k_t, v_s, lse, exact, mixed,
+        head_weights, misc_t, full_out, resid, moe_in, all_cot, all_routes, all_experts,
+    ) = start(
+        tokens[0], cotangent[0], w_gate, w_up, w_down, pieces, out_piece, route_rows, 1
+    )
+    mixed = mixed.reshape(2048, 128)
     token_rows = tokens[0].astype(F32)
-    resid = token_rows + jnp.dot(mixed_rows, full_out, preferred_element_type=F32)
-    moe_in = rms_scale(resid, gain_moe).astype(BF16)
+    full_router = misc_t[:32].T
+    gain_attn, gain_moe = misc_t[33:34], misc_t[32]
     all_moe = gather_exp(moe_in, 3)
     out_parts, grad_parts, rows, slot_grads, hidden, gate_grads, up_grads = experts(
-        exp.reshape(1).astype(jnp.int32), all_moe, all_cot, all_routes, router_t, all_experts
+        exp.reshape(1).astype(jnp.int32), all_moe, all_cot, all_routes, misc_t, all_experts
     )
     grad_total = reduce_exp(grad_parts, 4)
     expert_out = lax.psum_scatter(
@@ -792,7 +1164,7 @@
         .reshape(3, 2, 128, 512)
     )
 
-    logits = jnp.dot(moe_in, full_router, preferred_element_type=F32)
+    logits = jnp.dot(moe_in, full_router.astype(BF16), preferred_element_type=F32)
     chosen = jnp.any(
         routes[0][:, :, None] == jnp.arange(32, dtype=jnp.int32)[None, None, :], axis=1
     )
@@ -809,7 +1181,7 @@
     router_term = jnp.dot(moe_in.astype(F32).T, logit_grad, precision=PRECISE)
     moe_in_grad = grad_total[:, :ROWS].astype(F32).transpose(1, 0, 2).reshape(256, 1024)
     moe_in_grad = moe_in_grad + jnp.dot(
-        logit_grad, full_router.astype(F32).T, precision=PRECISE
+        logit_grad, misc_t[:32], precision=PRECISE
     )
     unused_moe, pull_moe = jax.vjp(rms_scale, resid, gain_moe)
     resid_grad, norm_moe_term = pull_moe(moe_in_grad)

time: 504 us -> 418 us (0.83)
  blocking collectives: 40.9 us -> 0 us
  Pallas kernels: 326 us -> 315 us
  local copies, waits for them, and re-layouts: 33.4 us -> 22.5 us
  matrix products: 36.9 us -> 28 us
  starting transfers between devices: 27.1 us -> 18.4 us
    pallas_call x3 -> x1, Pallas kernels: 109 us -> 30.6 us  [gather_ctx(): pl.pallas_call(gather_ctx_kernel, out_shape=jax.ShapeDtypeStruct((8,) + b...]
    pallas_call x1, Pallas kernels: 26.4 us -> 88.6 us  [start(): pl.pallas_call(start_kernel, out_shape=[jax.ShapeDtypeStruct(s, t) for s,...]
    all_gather x2 -> x0, blocking collectives: 40.9 us -> none  [the longest x1 21.4 us: per_device(): group_rows = lax.all_gather(narrow, 'exp', axis=0, tiled=True)]
    all_to_all x2 -> x0, starting transfers between devices: 14.6 us -> none  [the longest x1 10.5 us: per_device(): lax.all_to_all(by_head.transpose(1, 0, 2), 'ctx', split_axis=0, concat_ax...]
    all_to_all x1, starting transfers between devices: 4.9 us -> 11.6 us  [per_device(): lax.all_to_all(mixed_grad.reshape(256, 8, 128).transpose(1, 0, 2), 'ctx',...]
    reshape x5 -> x4, local copies, waits for them, and re-layouts: 7.6 us -> 1.58 us  [the longest x2 0.79 us: per_device(): w_key.reshape(8, 8, 64)]
    unnamed x65 -> x71, local copies, waits for them, and re-layouts: 11.8 us -> 9.59 us
  transfers between devices with their start and end apart: 8 -> 4, of which waited for: 1 -> 0; matrix products, arithmetic and copies ran while one was open for 9% -> 5% of each run, Pallas kernels for 57% -> 34%
where the time goes in v2:
time: 418 us; the launch traced here: 411 us
  Pallas kernels  315 us (75%)
  matrix products  28 us (7%)
  local copies, waits for them, and re-layouts  22.5 us (5%)
  starting transfers between devices  18.4 us (4%)
  between operations  15.2 us (4%)
  other arithmetic  11.2 us (3%)
    pallas_call x1, Pallas kernels, start(): pl.pallas_call(start_kernel, out_shape=[jax.ShapeDtypeStruct(s, t) for s,...  88.6 us
    pallas_call x2, Pallas kernels, reduce_exp(): pl.pallas_call(reduce_exp_kernel, out_shape=jax.ShapeDtypeStruct((quarter...  61.9 us
    pallas_call x1, Pallas kernels, gather_exp(): pl.pallas_call(gather_exp_kernel, out_shape=jax.ShapeDtypeStruct((16, row...  44.9 us
    pallas_call x1, Pallas kernels, experts(): pl.pallas_call(experts_kernel, grid_spec=pltpu.PrefetchScalarGridSpec(num...  42.3 us
    pallas_call x1, Pallas kernels, gather_ctx(): pl.pallas_call(gather_ctx_kernel, out_shape=jax.ShapeDtypeStruct((8,) + b...  30.6 us
    pallas_call x1, Pallas kernels, reduce_ctx(): pl.pallas_call(reduce_ctx_kernel, out_shape=jax.ShapeDtypeStruct((lines,...  26 us
    pallas_call x1, Pallas kernels, attend_back(): pl.pallas_call(attend_back_kernel, out_shape=jax.ShapeDtypeStruct((2048,...  20.4 us
    dot_general x3, matrix products, expert_term(): jnp.einsum('erd,erf->edf', left, right, preferred_element_type=F32)  19.3 us
  transfers between devices with their start and end apart: 4, of which 0 were waited for; matrix products, arithmetic and copies ran while one was open for 5% of the time, Pallas kernels for 34%

profile of v2, /device:TPU:1, one launch (start us, length us, event | category | flops | bytes accessed | tf_op | source)
XLA Modules:
  0.0 410.6 jit_solution(10574493484276705979)
XLA Ops:
  7.2 0.8 reshape.205
  8.0 0.8 reshape.206
  8.8 0.8 maximum_bitcast_fusion.1
  9.6 0.7 copy.107
  10.4 0.7 copy.108
  11.1 0.7 convert_bitcast_fusion.1
  11.8 0.6 pad.13.routes
  12.5 0.8 fusion.22
  13.3 0.7 maximum_maximum_fusion.pieces
  14.0 88.6 %shard_map.220 = (bf16[2048,1024]{1,0:T(8,128)(2,1)}, bf16[8,64,512]{2,1,0:T(8,128)(2,1)}, bf16[8,512,64]{2,1,0:T(8,128)(2,1)}, bf16[8,256,64]{2,1,0:T(8,128)(2,...) custom-call(bf16[256,1024]{1,0:T(8,128)(2,1)} %bitcast.144, ...), custom_call_target="tpu_custom_call" | custom-call | tf_op jit(solution)/shard_map/pallas_call | solution.py:1061
  102.6 44.9 %shard_map.221.moe = bf16[16,256,1024]{2,1,0:T(8,128)(2,1)} custom-call(bf16[256,1024]{1,0:T(8,128)(2,1)} %get-tuple-element.37.own), custom_call_target="tpu_custom_call" | custom-call | tf_op jit(solution)/shard_map/pallas_call | solution.py:105
  147.5 42.3 %shard_map.222 = (bf16[16,4,256,256]{3,2,1,0:T(8,128)(2,1)}, bf16[16,4,272,256]{3,2,1,0:T(8,128)(2,1)}, bf16[2,16,96,1024]{3,2,1,0:T(8,128)(2,1)}, bf16[2,16,96,...) custom-call(s32[1]{0:T(128)} %bitcast.14.owner, ...), custom_call_target="tpu_custom_call" | custom-call | tf_op jit(solution)/shard_map/pallas_call | solution.py:682
  189.8 7.3 %convolution_convert_fusion.2 = bf16[2,1024,512]{2,1,0:T(8,128)(2,1)S(1)} fusion(bf16[2,1536,1024]{2,1,0:T(8,128)(2,1)} %bitcast.178, bf16[2,1536,512]{2,1,0:T(8,128)(2,1)} %bitcast.182), kind=kOutput, calls=%fused_computation.10 | convolution fusion | flops 3222274048 | bytes 11534336 | tf_op jit(solution)/shard_map/erd,erf->edf/dot_general | solution.py:1150
  197.1 8.3 %convolution_convert_fusion.3 = bf16[2,1024,512]{2,1,0:T(8,128)(2,1)S(1)} fusion(bf16[2,1536,1024]{2,1,0:T(8,128)(2,1)} %bitcast.179, bf16[2,1536,512]{2,1,0:T(8,128)(2,1)S(1)} %bitcast.181), kind=kOutput, calls=%fused_computation.11 | convolution fusion | flops 3222274048 | bytes 11534336 | tf_op jit(solution)/shard_map/erd,erf->edf/dot_general | solution.py:1150
  205.7 1.7 copy-done.28
  207.3 3.7 convolution_convert_fusion.1
  211.0 0.4 copy_bitcast_fusion
  211.5 3.3 pad_maximum_fusion
  214.9 0.7 reduce-scatter.3.cloned.1.call-update
  215.6 3.5 copy-done
  219.1 49.2 %shard_map.223 = bf16[4,272,256]{2,1,0:T(8,128)(2,1)S(1)} custom-call(bf16[16,4,272,256]{3,2,1,0:T(8,128)(2,1)S(1)} %copy-done), custom_call_target="tpu_custom_call" | custom-call | tf_op jit(solution)/shard_map/pallas_call | solution.py:222
  268.7 0.3 copy-done.24
  270.0 1.4 multiply_reduce_fusion
  271.7 0.6 copy-done.8
  272.3 0.8 fusion.3
  273.1 0.9 copy.142
  274.0 11.6 %all-to-all-start = ((bf16[8,256,128]{2,1,0:T(8,128)(2,1)}), bf16[8,256,128]{2,1,0:T(8,128)(2,1)S(1)}, u32[]{:S(2)}, u32[]{:S(2)}) async-start(bf16[8,256,128]{2,1,0:T(8,128)(2,1)} %bitcast.135), calls=%async_computation.1 | async-start | bytes 1048576 | tf_op jit(solution)/shard_map/all_to_all | solution.py:1193
  285.7 30.6 %shard_map.226 = bf16[8,256,1024]{2,1,0:T(8,128)(2,1)} custom-call(bf16[256,1024]{1,0:T(8,128)(2,1)} %copy-done.15), custom_call_target="tpu_custom_call" | custom-call | tf_op jit(solution)/shard_map/pallas_call | solution.py:307
  316.3 3.3 fusion.4
  319.7 0.8 reshape_transpose_reshape.4
  320.5 0.3 convolution_convert_fusion.6
  321.0 0.4 concatenate.37
  321.7 0.3 reshape.221
  322.1 20.4 %shard_map.224 = bf16[2048,256]{1,0:T(8,128)(2,1)S(1)} custom-call(bf16[2048,128]{1,0:T(8,128)(2,1)S(1)} %bitcast.139, bf16[8,64,512]{2,1,0:T(8,128)(2,1)S(1)} %copy-done.1, bf16[8,512,64]{2,1,0:T(8,128)(2,1)} %get-tuple-element.46.q_s, bf16[8,256,64]{2,1,0:T(8,128)(2,1)S(1)} %copy-done.2, bf16[8,64,256]{2,1,0:T(8,128)(2,1)S(1)} %copy-done.4, ...), custom_call_target="tpu_custom_call" | custom-call | tf_op jit(solution)/shard_map/pallas_call | solution.py:546
  342.5 1.3 convolution_convert_fusion.5
  344.5 12.7 %shard_map.227 = bf16[4,32,256]{2,1,0:T(8,128)(2,1)S(1)} custom-call(bf16[16,4,32,256]{3,2,1,0:T(8,128)(2,1)S(1)} %bitcast.138), custom_call_target="tpu_custom_call" | custom-call | tf_op jit(solution)/shard_map/pallas_call | solution.py:222
  357.4 0.7 maximum_convert_fusion
  358.1 6.6 %all-to-all-start.1 = ((f32[8,8,289]{2,1,0:T(8,128)}), f32[8,8,289]{2,1,0:T(8,128)S(1)}, u32[]{:S(2)}, u32[]{:S(2)}) async-start(f32[8,8,289]{2,1,0:T(8,128)} %maximum_convert_fusion), calls=%async_computation.2 | async-start | bytes 196608 | tf_op jit(solution)/shard_map/all_to_all | solution.py:1221
  364.7 1.3 convolution_convert_fusion
  366.1 26.0 %shard_map.225 = bf16[256,1024]{1,0:T(8,128)(2,1)S(1)} custom-call(bf16[8,256,1024]{2,1,0:T(8,128)(2,1)S(1)} %bitcast.137), custom_call_target="tpu_custom_call" | custom-call | tf_op jit(solution)/shard_map/pallas_call | solution.py:378
  392.5 0.6 reshape.241
  393.4 0.7 slice_reduce_fusion.1
  394.3 0.7 multiply_reduce_fusion.3
  395.0 0.5 convert_divide_fusion
  395.5 2.3 fusion.26
  397.8 2.2 copy.126
  400.0 1.5 copy.109
  401.8 1.6 fusion.13
  (113 shorter events, 4.2 us)
Async XLA Ops:
  7.2 388.3 %reduce-scatter.5.cloned.1.call-start = ((), (), s32[]{:S(2)}) async-start(), calls=%async_computation.5 | async-start | bytes 7077888 | tf_op jit(solution)/shard_map/reduce_scatter | solution.py:1162
  189.8 7.3 %copy-start.29 = (bf16[2,16,96,512]{3,2,1,0:T(8,128)(2,1)S(1)}, bf16[2,16,96,512]{3,2,1,0:T(8,128)(2,1)}, u32[]{:S(2)}) copy-start(bf16[2,16,96,512]{3,2,1,0:T(8,128)(2,1)} %get-tuple-element.56) | copy-start | bytes 9437188
  189.8 15.8 %slice-start = ((s8[6291456]{0:T(1024)(128)(4,1)}), s8[4194304]{0:T(1024)(128)(4,1)S(1)}, s32[]{:S(2)}) async-start(s8[6291456]{0:T(1024)(128)(4,1)} %bitcast.175), calls=%async_computation.6 | async-start | bytes 8388608
  197.1 8.5 %slice-start.1 = ((s8[6291456]{0:T(1024)(128)(4,1)}), s8[2097152]{0:T(1024)(128)(4,1)S(1)}, s32[]{:S(2)}) async-start(s8[6291456]{0:T(1024)(128)(4,1)} %bitcast.175), calls=%async_computation.7 | async-start | bytes 4194304
  205.4 1.9 copy-start.28
  214.8 185.2 %reduce-scatter.3.cloned.1.call-start = ((), (), s32[]{:S(2)}) async-start(), calls=%async_computation.4 | async-start | bytes 8912896 | tf_op jit(solution)/shard_map/reduce_scatter | solution.py:1139
  215.6 3.5 copy-start
  268.3 0.7 copy-start.24
  268.4 1.0 copy-start.10
  268.4 1.1 copy-start.16
  268.4 1.4 copy-start.6
  268.7 2.7 copy-start.13
  270.0 2.3 copy-start.30
  271.3 1.0 copy-start.8
  272.3 13.4 %copy-start.15 = (bf16[256,1024]{1,0:T(8,128)(2,1)}, bf16[256,1024]{1,0:T(8,128)(2,1)S(1)}, u32[]{:S(2)}) copy-start(bf16[256,1024]{1,0:T(8,128)(2,1)S(1)} %fusion.25.own) | copy-start | bytes 1572868
  274.0 48.0 %all-to-all-start = ((bf16[8,256,128]{2,1,0:T(8,128)(2,1)}), bf16[8,256,128]{2,1,0:T(8,128)(2,1)S(1)}, u32[]{:S(2)}, u32[]{:S(2)}) async-start(bf16[8,256,128]{2,1,0:T(8,128)(2,1)} %bitcast.135), calls=%async_computation.1 | async-start | bytes 1048576 | tf_op jit(solution)/shard_map/all_to_all | solution.py:1193
  316.3 4.2 %copy-start.11 = (bf16[256,1024]{1,0:T(8,128)(2,1)S(1)}, bf16[256,1024]{1,0:T(8,128)(2,1)}, u32[]{:S(2)}) copy-start(bf16[256,1024]{1,0:T(8,128)(2,1)} %get-tuple-element.37.own) | copy-start | bytes 1572868
  316.3 5.8 %copy-start.1 = (bf16[8,64,512]{2,1,0:T(8,128)(2,1)S(1)}, bf16[8,64,512]{2,1,0:T(8,128)(2,1)}, u32[]{:S(2)}) copy-start(bf16[8,64,512]{2,1,0:T(8,128)(2,1)} %get-tuple-element.45.q_t) | copy-start | bytes 1572868
  316.3 5.8 %copy-start.2 = (bf16[8,256,64]{2,1,0:T(8,128)(2,1)S(1)}, bf16[8,256,64]{2,1,0:T(8,128)(2,1)}, u32[]{:S(2)}) copy-start(bf16[8,256,64]{2,1,0:T(8,128)(2,1)} %get-tuple-element.47.k_s) | copy-start | bytes 786436
  316.3 5.8 %copy-start.3 = (bf16[8,256,64]{2,1,0:T(8,128)(2,1)S(1)}, bf16[8,256,64]{2,1,0:T(8,128)(2,1)}, u32[]{:S(2)}) copy-start(bf16[8,256,64]{2,1,0:T(8,128)(2,1)} %get-tuple-element.49.v_s) | copy-start | bytes 786436
  316.3 5.8 %copy-start.4 = (bf16[8,64,256]{2,1,0:T(8,128)(2,1)S(1)}, bf16[8,64,256]{2,1,0:T(8,128)(2,1)}, u32[]{:S(2)}) copy-start(bf16[8,64,256]{2,1,0:T(8,128)(2,1)} %get-tuple-element.48.k_t) | copy-start | bytes 786436
  316.3 5.8 %copy-start.5 = (f32[8,1,512]{2,1,0:T(1,128)S(1)}, f32[8,1,512]{2,1,0:T(1,128)}, u32[]{:S(2)}) copy-start(f32[8,1,512]{2,1,0:T(1,128)} %get-tuple-element.50.lse) | copy-start | bytes 49156
  322.1 20.5 %copy-start.27 = (bf16[2048,1024]{1,0:T(8,128)(2,1)S(1)}, bf16[2048,1024]{1,0:T(8,128)(2,1)}, u32[]{:S(2)}) copy-start(bf16[2048,1024]{1,0:T(8,128)(2,1)} %get-tuple-element.53) | copy-start | bytes 12582916
  342.5 1.7 copy-start.17
  343.9 20.8 %copy-start.18 = (bf16[1024,256]{1,0:T(8,128)(2,1)S(1)}, bf16[1024,256]{1,0:T(8,128)(2,1)}, u32[]{:S(2)}) copy-start(bf16[1024,256]{1,0:T(8,128)(2,1)} %get-tuple-element.52) | copy-start | bytes 1572868
  358.1 35.0 %all-to-all-start.1 = ((f32[8,8,289]{2,1,0:T(8,128)}), f32[8,8,289]{2,1,0:T(8,128)S(1)}, u32[]{:S(2)}, u32[]{:S(2)}) async-start(f32[8,8,289]{2,1,0:T(8,128)} %maximum_convert_fusion), calls=%async_computation.2 | async-start | bytes 196608 | tf_op jit(solution)/shard_map/all_to_all | solution.py:1221
  366.0 26.1 %copy-start.12 = (bf16[1,256,1024]{2,1,0:T(8,128)(2,1)S(1)}, bf16[1,256,1024]{2,1,0:T(8,128)(2,1)}, u32[]{:S(2)}) copy-start(bf16[1,256,1024]{2,1,0:T(8,128)(2,1)} %param.13) | copy-start | bytes 1572868
  366.0 28.1 %copy-start.22 = (bf16[8,512]{1,0:T(8,128)(2,1)S(1)}, bf16[8,512]{1,0:T(8,128)(2,1)}, u32[]{:S(2)}) copy-start(bf16[8,512]{1,0:T(8,128)(2,1)} %param.17) | copy-start | bytes 24580
  366.1 28.0 %copy-start.23 = (bf16[8,512]{1,0:T(8,128)(2,1)S(1)}, bf16[8,512]{1,0:T(8,128)(2,1)}, u32[]{:S(2)}) copy-start(bf16[8,512]{1,0:T(8,128)(2,1)} %param.16) | copy-start | bytes 24580
  366.1 28.2 %copy-start.19 = (bf16[8,1024]{1,0:T(8,128)(2,1)S(1)}, bf16[8,1024]{1,0:T(8,128)(2,1)}, u32[]{:S(2)}) copy-start(bf16[8,1024]{1,0:T(8,128)(2,1)} %param.15) | copy-start | bytes 49156
  366.1 28.9 %copy-start.26 = (bf16[8]{0:T(256)(128)(2,1)S(1)}, bf16[8]{0:T(256)(128)(2,1)}, u32[]{:S(2)}) copy-start(bf16[8]{0:T(256)(128)(2,1)} %param.14) | copy-start | bytes 52
  393.3 8.4 %copy-start.20 = (f32[8,512]{1,0:T(8,128)}, f32[8,512]{1,0:T(8,128)S(1)}, u32[]{:S(2)}) copy-start(f32[8,512]{1,0:T(8,128)S(1)} %reshape.225) | copy-start | bytes 49156
  393.4 8.4 %copy-start.21 = (f32[8,512]{1,0:T(8,128)}, f32[8,512]{1,0:T(8,128)S(1)}, u32[]{:S(2)}) copy-start(f32[8,512]{1,0:T(8,128)S(1)} %reshape.226) | copy-start | bytes 49156
  393.4 8.4 %copy-start.25 = (f32[8,33]{1,0:T(8,128)}, f32[8,33]{1,0:T(8,128)S(1)}, u32[]{:S(2)}) copy-start(f32[8,33]{1,0:T(8,128)S(1)} %slice_reduce_fusion) | copy-start | bytes 3172
  397.8 3.9 copy-start.7
  397.8 3.9 copy-start.9
  400.0 1.8 copy-start.14
Sparse Core Ops, SparseCore 0:
  214.9 45.1 reduce-scatter.4
  263.5 84.4 reduce-scatter.2
